TPU v7x, 128 devices: a whole 4x4x4 slice. The times are simulated.
128 devices in a mesh: cluster: 8 (over y, core), shard: 16 (over z, x).
Axes of the slice: x: 4, y: 4, z: 4, core: 2. Of those that a mesh axis runs over, the one named last changes fastest.
Arguments:
- documents: bfloat16 [65536, 1024], P(('cluster', 'shard'))
- partners: int32 [128, 4], P(('cluster', 'shard')), may hold values from 0 to 31, as said below
- counts: int32 [128], P(('cluster', 'shard')), may hold values from 64 to 512
Outputs:
- nearest: float32 [65536], P(('cluster', 'shard'))
Inputs may be any that keep to these rules, and one draw needn't show every extreme that they name: partners[k, 0] = k mod 16, a block's pair with itself; every code names a block of its own group (below 16) or of the next group in cyclic order.
All inputs are finite; a program needn't handle non-finite values.
Results may differ from a plain program's by a relative error of at most 0.00063.
Values may be sent and summed in bfloat16 or wider, within the bound.
No kernel may reach another device: no remote copies, remote signals or barrier semaphores. Data moves between devices by JAX's collectives and lax.ppermute only.
A program may use at most 128 MiB of HBM per device.

v0:
```python
import jax
import jax.numpy as jnp
from jax import lax
from jax.sharding import PartitionSpec as P

ROWS = 512
PAIRS = 4


def with_halo(x, sides, width):
    for axis, dim in sides:
        size, length = (lax.axis_size(axis), x.shape[dim])
        up = [(i, (i + 1) % size) for i in range(size)]
        down = [(j, i) for i, j in up]
        last = lax.slice_in_dim(x, length - width, length, axis=dim)
        first = lax.slice_in_dim(x, 0, width, axis=dim)
        before = lax.ppermute(last, axis, up)
        after = lax.ppermute(first, axis, down)
        x = jnp.concatenate([before, x, after], axis=dim)
    return x


def shards(documents, partners, counts):
    n_shard = lax.axis_size("shard")
    n_cluster = lax.axis_size("cluster")
    my_cluster = lax.axis_index("cluster")
    my_shard = lax.axis_index("shard")
    mine = my_cluster * n_shard + my_shard
    raw = documents.astype(jnp.float32)
    inv = lax.rsqrt(jnp.sum(raw * raw, axis=1, keepdims=True) + 1e-06)
    unit = (raw * inv).astype(jnp.bfloat16)
    own_row = jnp.concatenate([partners, counts[:, None]], axis=1)
    group_table = lax.all_gather(own_row, "shard", axis=0, tiled=True)
    slots = jnp.arange(ROWS, dtype=jnp.int32)
    row_ok = slots < counts[0]
    shard_ids = jnp.arange(n_shard, dtype=jnp.int32)
    table3 = with_halo(group_table[None], (("cluster", 0),), 1)
    near_groups = (my_cluster + jnp.arange(3, dtype=jnp.int32) - 1) % n_cluster
    parts3 = table3[:, :, :PAIRS]
    counts3 = table3[:, :, PAIRS]
    grp3 = near_groups[:, None, None]
    target3 = jnp.where(
        parts3 < n_shard,
        grp3 * n_shard + parts3,
        (grp3 + 1) % n_cluster * n_shard + parts3 - n_shard,
    )
    base3 = near_groups * n_shard
    block3 = base3[:, None] + shard_ids[None, :]
    my_targets = lax.dynamic_index_in_dim(target3[1], my_shard, 0, keepdims=False)
    listed3 = jnp.logical_or(
        jnp.any(block3[:, :, None] == my_targets[None, None, :], axis=2),
        jnp.any(target3 == mine, axis=2),
    )
    stacked = with_halo(unit[None], (("cluster", 0),), 1)
    piece = lax.all_gather(stacked, "shard", axis=1, tiled=True)
    width = piece.shape[1]
    scores = jnp.einsum("rd,gmd->rgm", unit, piece, preferred_element_type=jnp.float32)
    column = jnp.arange(width, dtype=jnp.int32)
    owner_shard = column // ROWS
    local = column % ROWS
    onehot = owner_shard[:, None] == shard_ids[None, :]
    col_listed = jnp.any(jnp.logical_and(onehot[None], listed3[:, None, :]), axis=2)
    col_count = jnp.sum(jnp.where(onehot[None], counts3[:, None, :], 0), axis=2)
    self_block = base3[:, None] + owner_shard[None, :] == mine
    keep = jnp.logical_and(col_listed, local[None, :] < col_count)
    same = jnp.logical_and(self_block[None], local[None, None, :] == slots[:, None, None])
    keep = jnp.logical_and(keep[None], jnp.logical_not(same))
    best = jnp.maximum(
        jnp.full((ROWS,), -1.0, jnp.float32), jnp.max(jnp.where(keep, scores, -1.0), axis=(1, 2))
    )
    return jnp.where(row_ok, best, 0.0)


def solution(mesh):
    return jax.shard_map(
        shards,
        mesh=mesh,
        in_specs=(
            P(("cluster", "shard"), None),
            P(("cluster", "shard"), None),
            P(("cluster", "shard")),
        ),
        out_specs=P(("cluster", "shard")),
        check_vma=False,
    )
```

profile of v0, /device:TPU:0, one launch (start us, length us, event | category | flops | bytes accessed | tf_op | source)
XLA Modules:
  0.0 355.5 jit_solution(6981947583602619381)
XLA Ops:
  6.5 1.5 fusion
  8.0 1.5 fusion.4
  9.5 0.0 copy-start.1
  9.5 2.5 collective-permute-start.3
  12.1 12.3 %collective-permute-done.3 = bf16[1,512,1024]{2,1,0:T(8,128)(2,1)S(1)} collective-permute-done((bf16[1,512,1024]{2,1,0:T(8,128)(2,1)S(1)}, bf16[1,512,1024]{2,1,0:T(8,128)(2,1)S(1)}, u32[]{:S(2)}, u32[]{:S(2)}) %collective-permute-start.3) | collective-permute-done | bytes 1048608 | tf_op jit(solution)/shard_map/ppermute | solution.py:18
  24.4 3.1 collective-permute-done.2
  27.5 2.0 pad_maximum_fusion
  29.5 0.0 all-gather.3.cloned.1.call-update
  30.3 0.1 add_bitcast_fusion.1
  30.3 21.9 %all-gather = s32[16,1,5]{2,1,0:T(1,128)S(1)} all-gather(s32[1,1,5]{2,1,0:T(1,128)S(1)} %add_bitcast_fusion.1), channel_id=1, replica_groups=mesh['cluster'=8,'shard'=16] {'shard'}, dimensions={0}, use_global_device_ids=true | all-gather | bytes 340 | tf_op jit(solution)/shard_map/all_gather | solution.py:33
  52.2 0.1 copy.7
  52.3 0.5 collective-permute-start
  52.9 0.1 iota_add_fusion
  53.0 0.1 iota_compare_fusion.1
  53.0 4.5 %iota_compare_fusion = pred[512,8192]{1,0:T(8,128)(4,1)} fusion(s32[8192]{0:T(1024)S(1)} %fusion.5), kind=kLoop, calls=%fused_computation.1 | loop fusion | flops 4194304 | bytes 4227072 | tf_op jit(solution)/shard_map/eq | solution.py:66
  57.6 0.1 compare_reduce_fusion
  57.7 0.2 dynamic-slice_reduce_fusion
  57.9 0.1 compare_reduce_fusion.1
  58.0 0.4 and_reduce_fusion
  58.4 0.4 select_reduce_fusion.1
  58.8 0.1 add_compare_fusion
  58.9 253.5 %all-gather.3.cloned.1.call-done = bf16[3,8192,1024]{2,1,0:T(8,128)(2,1)} async-done(((bf16[3,512,1024]{2,1,0:T(8,128)(2,1)}), bf16[3,8192,1024]{2,1,0:T(8,128)(2,1)}) %all-gather.3.cloned.1.call-update) | async-done | bytes 50331664 | tf_op jit(solution)/shard_map/all_gather | solution.py:55
  312.4 35.6 %select_reduce_fusion = f32[512]{0:T(512)S(1)} fusion(pred[512,8192]{1,0:T(8,128)(4,1)} %iota_compare_fusion, pred[3,8192]{1,0:T(4,128)(4,1)S(1)} %get-tuple-element.7, pred[3,8192]{1,0:T(4,128)(4,1)S(1)} %get-tuple-element.8, bf16[3,8192,1024]{2,1,0:T(8,128)(2,1)} %all-gather.3.cloned.1.call-done, bf16[512,1024]{1,0:T(8,128)(2,1)S(1)} %copy-done, ...), kind=kOutput, calls=%fused_computation | convolution fusion | flops 25834291200 | bytes 55627776 | tf_op jit(solution)/shard_map/rd,gmd->rgm/dot_general | solution.py:57
  348.0 0.6 maximum_select_fusion
  (17 shorter events, 0.1 us)
Async XLA Ops:
  6.5 305.9 %all-gather.3.cloned.1.call-start = ((), (), s32[]{:S(2)}) async-start(), calls=%async_computation | async-start | bytes 53477376 | tf_op jit(solution)/shard_map/all_gather | solution.py:55
  9.5 20.7 %copy-start.1 = (s32[1,4]{1,0:T(1,128)S(1)}, s32[1,4]{1,0:T(1,128)}, u32[]{:S(2)}) copy-start(s32[1,4]{1,0:T(1,128)} %param.4) | copy-start | bytes 52
  9.5 14.9 %collective-permute-start.3 = (bf16[1,512,1024]{2,1,0:T(8,128)(2,1)S(1)}, bf16[1,512,1024]{2,1,0:T(8,128)(2,1)S(1)}, u32[]{:S(2)}, u32[]{:S(2)}) collective-permute-start(bf16[1,512,1024]{2,1,0:T(8,128)(2,1)S(1)} %fusion.4), channel_id=1, source_target_pairs={{16,0},{32,16},{48,32},{64,48},{80,64},{96,80},{112,96},{0,112},{1... | collective-permute-start | bytes 3145736 | tf_op jit(solution)/shard_map/ppermute | solution.py:18
  12.1 15.4 %collective-permute-start.2 = (bf16[1,512,1024]{2,1,0:T(8,128)(2,1)S(1)}, bf16[1,512,1024]{2,1,0:T(8,128)(2,1)S(1)}, u32[]{:S(2)}, u32[]{:S(2)}) collective-permute-start(bf16[1,512,1024]{2,1,0:T(8,128)(2,1)S(1)} %fusion.4), channel_id=1, source_target_pairs={{0,16},{16,32},{32,48},{48,64},{64,80},{80,96},{96,112},{112,0},{1... | collective-permute-start | bytes 3145736 | tf_op jit(solution)/shard_map/ppermute | solution.py:17
  29.5 282.9 %copy-start = (bf16[512,1024]{1,0:T(8,128)(2,1)S(1)}, bf16[512,1024]{1,0:T(8,128)(2,1)}, u32[]{:S(2)}) copy-start(bf16[512,1024]{1,0:T(8,128)(2,1)} %param.3) | copy-start | bytes 3145732
  52.3 5.3 %collective-permute-start.1 = (s32[1,16,5]{1,0,2:T(1,128)S(1)}, s32[1,16,5]{1,0,2:T(1,128)S(1)}, u32[]{:S(2)}, u32[]{:S(2)}) collective-permute-start(s32[1,16,5]{1,0,2:T(1,128)S(1)} %bitcast.15), channel_id=1, source_target_pairs={{16,0},{32,16},{48,32},{64,48},{80,64},{96,80},{112,96},{0,112},{1... | collective-permute-start | bytes 968 | tf_op jit(solution)/shard_map/ppermute | solution.py:18
  52.3 5.3 %collective-permute-start = (s32[1,16,5]{1,0,2:T(1,128)S(1)}, s32[1,16,5]{1,0,2:T(1,128)S(1)}, u32[]{:S(2)}, u32[]{:S(2)}) collective-permute-start(s32[1,16,5]{1,0,2:T(1,128)S(1)} %bitcast.16), channel_id=1, source_target_pairs={{0,16},{16,32},{32,48},{48,64},{64,80},{80,96},{96,112},{112,0},{1... | collective-permute-start | bytes 968 | tf_op jit(solution)/shard_map/ppermute | solution.py:17
Sparse Core Ops, SparseCore 0:
  29.6 282.7 all-gather.2
where the time goes:
time: 356 us; the launch traced here: 355 us
  waiting for transfers between devices  269 us (76%)
  matrix products  35.6 us (10%)
  blocking collectives  21.9 us (6%)
  between operations  14.2 us (4%)
  other arithmetic  11.4 us (3%)
    all_gather x1, waiting for transfers between devices, shards(): piece = lax.all_gather(stacked, 'shard', axis=1, tiled=True)  253 us
    dot_general x1, matrix products, shards(): jnp.einsum('rd,gmd->rgm', unit, piece, preferred_element_type=jnp.float32)  35.6 us
    all_gather x1, blocking collectives, shards(): group_table = lax.all_gather(own_row, 'shard', axis=0, tiled=True)  21.9 us
    ppermute x2, waiting for transfers between devices, with_halo(): after = lax.ppermute(first, axis, down)  12.3 us
  transfers between devices with their start and end apart: 5, of which 3 were waited for; matrix products, arithmetic and copies ran while one was open for 2% of the time, Pallas kernels for 0%

commit v1 on v0

v1 whole, which is shorter than its diff:
```python
import functools

import jax
import jax.numpy as jnp
from jax import lax
from jax.experimental import pallas as pl
from jax.experimental.pallas import tpu as pltpu
from jax.sharding import PartitionSpec as P

ROWS = 512
D = 1024
PAIRS = 4
SLOTS = PAIRS - 1
GROUP = 16
CUT = ROWS // GROUP
WIDE = D + 128
VMEM = pl.BlockSpec(memory_space=pltpu.VMEM)
SMEM = pl.BlockSpec(memory_space=pltpu.SMEM)


def normalise(doc_ref, row_ref, out_ref):
    raw = doc_ref[...].astype(jnp.float32)
    inv = lax.rsqrt(jnp.sum(raw * raw, axis=1, keepdims=True) + 1e-06)
    out_ref[:, :D] = (raw * inv).astype(jnp.bfloat16)
    out_ref[:, D:] = jnp.broadcast_to(row_ref[...], (doc_ref.shape[0], WIDE - D)).astype(jnp.bfloat16)


def pick(code_ref, own_ref, next_ref, out_ref):
    def one(e, carry):
        code = code_ref[e]
        dst, slot = e // SLOTS, e % SLOTS

        @pl.when(code < GROUP)
        def _():
            out_ref[dst, slot] = own_ref[code, :, :D]

        @pl.when(code >= GROUP)
        def _():
            out_ref[dst, slot] = next_ref[code - GROUP, :, :D]

        return carry

    lax.fori_loop(0, GROUP * SLOTS, one, 0)


def pair_scores(info_ref, unit_ref, got_ref, best_ref, send_ref):
    mine, count = info_ref[0], info_ref[1]
    unit = unit_ref[:, :D]
    row = lax.broadcasted_iota(jnp.int32, (ROWS, 1), 0)
    col = lax.broadcasted_iota(jnp.int32, (1, ROWS), 1)
    row_ok = row < count
    send_ref[...] = jnp.full(send_ref.shape, -1.0, jnp.float32)
    part = jnp.full((ROWS, 128), -1.0, jnp.float32)
    for p in range(SLOTS + 1):
        if p == 0:
            other, code, other_count = unit, mine, count
        else:
            other = got_ref[:, p - 1].reshape(ROWS, D)
            code, other_count = info_ref[1 + p], info_ref[4 + p]
        scores = lax.dot_general(unit, other, (((1,), (1,)), ((), ())), preferred_element_type=jnp.float32)
        off = jnp.where(code == mine, 0, ROWS)
        scores = jnp.where(row + off == col, -1.0, scores)
        rows = jnp.where(col < other_count, scores, -1.0)
        for t in range(ROWS // 128):
            part = jnp.maximum(part, rows[:, t * 128 : (t + 1) * 128])
        if p > 0:
            cols = jnp.max(jnp.where(row_ok, scores, -1.0), axis=0, keepdims=True)
            dst, step = code % GROUP, code // GROUP
            held = send_ref[dst, pl.ds(step, 1), :]
            send_ref[dst, pl.ds(step, 1), :] = jnp.maximum(held, cols)
    best_ref[...] = jnp.max(part.T, axis=0, keepdims=True)


def shards(documents, partners, counts):
    n_cluster = lax.axis_size("cluster")
    my_shard = lax.axis_index("shard")
    down = [((j + 1) % n_cluster, j) for j in range(n_cluster)]
    up = [(j, (j + 1) % n_cluster) for j in range(n_cluster)]
    table = jnp.concatenate([partners[0], counts // 32, counts % 32]).astype(jnp.float32)
    table = jnp.pad(table, (0, WIDE - D - table.shape[0]))[None]
    step = 128
    unit = pl.pallas_call(
        normalise,
        grid=(ROWS // step,),
        in_specs=[pl.BlockSpec((step, D), lambda i: (i, 0)), pl.BlockSpec((1, WIDE - D), lambda i: (0, 0))],
        out_specs=pl.BlockSpec((step, WIDE), lambda i: (i, 0)),
        out_shape=jax.ShapeDtypeStruct((ROWS, WIDE), jnp.bfloat16),
    )(documents, table)
    own = lax.all_to_all(unit.reshape(GROUP, CUT, WIDE), "shard", 0, 0, tiled=True)
    nxt = lax.ppermute(own, "cluster", down)
    own_table = own[:, 0, D : D + 8].astype(jnp.int32)
    next_table = nxt[:, 0, D : D + 8].astype(jnp.int32)
    codes = own_table[:, 1:PAIRS].reshape(-1)
    picked = pl.pallas_call(
        pick,
        in_specs=[SMEM, VMEM, VMEM],
        out_specs=VMEM,
        out_shape=jax.ShapeDtypeStruct((GROUP, SLOTS, CUT, D), jnp.bfloat16),
        compiler_params=pltpu.CompilerParams(vmem_limit_bytes=32 * 2**20),
    )(codes, own, nxt)
    got = lax.all_to_all(picked, "shard", 0, 0, tiled=True)
    all_counts = jnp.concatenate([own_table, next_table])
    all_counts = all_counts[:, PAIRS] * 32 + all_counts[:, PAIRS + 1]
    mine = partners[0, 1:]
    info = jnp.concatenate([my_shard[None], counts, mine, all_counts[mine]]).astype(jnp.int32)
    best, send = pl.pallas_call(
        pair_scores,
        in_specs=[SMEM, VMEM, VMEM],
        out_specs=[VMEM, VMEM],
        out_shape=[
            jax.ShapeDtypeStruct((1, ROWS), jnp.float32),
            jax.ShapeDtypeStruct((GROUP, 2, ROWS), jnp.float32),
        ],
        compiler_params=pltpu.CompilerParams(vmem_limit_bytes=48 * 2**20),
    )(info, unit, got)
    back = jnp.max(lax.all_to_all(send, "shard", 0, 0, tiled=True), axis=0)
    before = lax.ppermute(back[1], "cluster", up)
    best = jnp.maximum(jnp.maximum(best[0], back[0]), before)
    return jnp.where(jnp.arange(ROWS, dtype=jnp.int32) < counts[0], best, 0.0)


def solution(mesh):
    return jax.shard_map(
        shards,
        mesh=mesh,
        in_specs=(
            P(("cluster", "shard"), None),
            P(("cluster", "shard"), None),
            P(("cluster", "shard")),
        ),
        out_specs=P(("cluster", "shard")),
        check_vma=False,
    )
```

time: 356 us -> 127 us (0.36)
  waiting for transfers between devices: 269 us -> 66.1 us
  matrix products: 35.6 us -> 0 us
  blocking collectives: 21.9 us -> 38.8 us
  between operations: 14.2 us -> 0.76 us
  other arithmetic: 11.4 us -> 2.38 us
  Pallas kernels: 0 us -> 8.79 us
  local copies, waits for them, and re-layouts: 0.32 us -> 4.46 us
    all_gather x1 -> x0, waiting for transfers between devices: 253 us -> none  [shards(): piece = lax.all_gather(stacked, 'shard', axis=1, tiled=True)]
    all_to_all x0 -> x1, waiting for transfers between devices: none -> 48.4 us  [shards(): got = lax.all_to_all(picked, 'shard', 0, 0, tiled=True)]
    all_to_all x0 -> x2, blocking collectives: none -> 38.8 us  [the longest x1 26.5 us: shards(): lax.all_to_all(unit.reshape(GROUP, CUT, WIDE), 'shard', 0, 0, tiled=True)]
    dot_general x1 -> x0, matrix products: 35.6 us -> none  [shards(): jnp.einsum('rd,gmd->rgm', unit, piece, preferred_element_type=jnp.float32)]
    all_gather x1 -> x0, blocking collectives: 21.9 us -> none  [shards(): group_table = lax.all_gather(own_row, 'shard', axis=0, tiled=True)]
    pallas_call x0 -> x3, Pallas kernels: none -> 8.79 us  [the longest x1 3.61 us: shards(): pl.pallas_call(normalise, grid=(ROWS // step,), in_specs=[pl.BlockSpec((s...]
    eq x3 -> x0, other arithmetic: 4.72 us -> none  [the longest x1 4.54 us: shards(): local[None, None, :] == slots[:, None, None]]
    all_to_all x0 -> x1, starting transfers between devices: none -> 3.87 us  [shards(): got = lax.all_to_all(picked, 'shard', 0, 0, tiled=True)]
  transfers between devices with their start and end apart: 5 -> 3, of which waited for: 3 -> 3; matrix products, arithmetic and copies ran while one was open for 2% -> 2% of each run, Pallas kernels for 0% -> 0%
where the time goes in v1:
time: 127 us; the launch traced here: 126 us
  waiting for transfers between devices  66.1 us (52%)
  blocking collectives  38.8 us (31%)
  Pallas kernels  8.79 us (7%)
  starting transfers between devices  4.93 us (4%)
  local copies, waits for them, and re-layouts  4.46 us (4%)
  other arithmetic  2.38 us (2%)
    all_to_all x1, waiting for transfers between devices, shards(): got = lax.all_to_all(picked, 'shard', 0, 0, tiled=True)  48.4 us
    all_to_all x1, blocking collectives, shards(): lax.all_to_all(unit.reshape(GROUP, CUT, WIDE), 'shard', 0, 0, tiled=True)  26.5 us
    ppermute x1, waiting for transfers between devices, shards(): nxt = lax.ppermute(own, 'cluster', down)  13.5 us
    all_to_all x1, blocking collectives, shards(): back = jnp.max(lax.all_to_all(send, 'shard', 0, 0, tiled=True), axis=0)  12.3 us
    ppermute x1, waiting for transfers between devices, shards(): before = lax.ppermute(back[1], 'cluster', up)  4.21 us
    all_to_all x1, starting transfers between devices, shards(): got = lax.all_to_all(picked, 'shard', 0, 0, tiled=True)  3.87 us
    pallas_call x1, Pallas kernels, shards(): pl.pallas_call(normalise, grid=(ROWS // step,), in_specs=[pl.BlockSpec((s...  3.61 us
    pallas_call x1, Pallas kernels, shards(): pl.pallas_call(pair_scores, in_specs=[SMEM, VMEM, VMEM], out_specs=[VMEM,...  3.32 us
  transfers between devices with their start and end apart: 3, of which 3 were waited for; matrix products, arithmetic and copies ran while one was open for 2% of the time, Pallas kernels for 0%

profile of v1, /device:TPU:0, one launch (start us, length us, event | category | flops | bytes accessed | tf_op | source)
XLA Modules:
  0.0 126.2 jit_solution(15649812669794213770)
XLA Ops:
  0.7 0.7 add_convert_fusion
  1.4 0.5 pad_bitcast_fusion.row_ref
  1.9 3.6 %shard_map.37.unit_ref = bf16[512,1152]{1,0:T(8,128)(2,1)} custom-call(bf16[512,1024]{1,0:T(8,128)(2,1)} %doc_ref.1, f32[1,128]{1,0:T(1,128)} %pad_bitcast_fusion.row_ref), custom_call_target="tpu_custom_call" | custom-call | tf_op jit(solution)/shard_map/pallas_call | solution.py:82
  5.5 26.5 %all_to_all.15.own_ref = bf16[16,32,1152]{2,1,0:T(8,128)(2,1)S(1)} all-to-all(bf16[16,32,1152]{2,1,0:T(8,128)(2,1)} %bitcast.19), channel_id=1, replica_groups=mesh['cluster'=8,'shard'=16] {'shard'}, dimensions={0} | all-to-all | bytes 2359296 | tf_op jit(solution)/shard_map/all_to_all | solution.py:89
  32.1 1.0 collective-permute-start
  33.2 0.1 copy.12
  33.3 0.1 reshape.47.code_ref
  33.4 13.5 %collective-permute-done.next_ref = bf16[16,32,1152]{2,1,0:T(8,128)(2,1)S(1)} collective-permute-done((bf16[16,32,1152]{2,1,0:T(8,128)(2,1)S(1)}, bf16[16,32,1152]{2,1,0:T(8,128)(2,1)S(1)}, u32[]{:S(2)}, u32[]{:S(2)}) %collective-permute-start) | collective-permute-done | bytes 1179680 | tf_op jit(solution)/shard_map/ppermute | solution.py:90
  46.8 1.9 %shard_map.38 = bf16[16,3,32,1024]{3,2,1,0:T(8,128)(2,1)S(1)} custom-call(s32[48]{0:T(128)S(1)} %reshape.47.code_ref, bf16[16,32,1152]{2,1,0:T(8,128)(2,1)S(1)} %all_to_all.15.own_ref, bf16[16,32,1152]{2,1,0:T(8,128)(2,1)S(1)} %collective-permute-done.next_ref), custom_call_target="tpu_custom_call" | custom-call | tf_op jit(solution)/shard_map/pallas_call | solution.py:94
  48.7 1.6 %copy-done = bf16[16,3,32,1024]{3,2,1,0:T(8,128)(2,1)} copy-done((bf16[16,3,32,1024]{3,2,1,0:T(8,128)(2,1)}, bf16[16,3,32,1024]{3,2,1,0:T(8,128)(2,1)S(1)}, u32[]{:S(2)}) %copy-start) | copy-done | bytes 3145752
  50.3 3.9 %all-to-all-start.1 = ((bf16[16,3,32,1024]{3,2,1,0:T(8,128)(2,1)}), bf16[16,3,32,1024]{3,2,1,0:T(8,128)(2,1)S(1)}, u32[]{:S(2)}, u32[]{:S(2)}) async-start(bf16[16,3,32,1024]{3,2,1,0:T(8,128)(2,1)} %copy-done), calls=%async_computation.1 | async-start | bytes 6291456 | tf_op jit(solution)/shard_map/all_to_all | solution.py:101
  54.2 0.1 fusion
  54.3 0.1 slice_bitcast_fusion
  54.4 0.8 slice_convert_fusion
  55.2 0.1 copy.11
  55.2 0.1 pad_add_fusion
  55.3 0.6 gather_fusion
  56.0 0.1 pad_add_fusion.1.info_ref
  56.0 48.4 %all-to-all-done.1.got_ref = bf16[16,3,32,1024]{3,2,1,0:T(8,128)(2,1)S(1)} async-done(((bf16[16,3,32,1024]{3,2,1,0:T(8,128)(2,1)}), bf16[16,3,32,1024]{3,2,1,0:T(8,128)(2,1)S(1)}, u32[]{:S(2)}, u32[]{:S(2)}) %all-to-all-start.1) | async-done | bytes 3145760 | tf_op jit(solution)/shard_map/all_to_all | solution.py:101
  104.5 1.3 %copy-done.1 = bf16[512,1152]{1,0:T(8,128)(2,1)S(1)} copy-done((bf16[512,1152]{1,0:T(8,128)(2,1)S(1)}, bf16[512,1152]{1,0:T(8,128)(2,1)}, u32[]{:S(2)}) %copy-start.1) | copy-done | bytes 1179672
  105.7 3.3 %shard_map.39 = (f32[1,512]{1,0:T(1,128)S(1)}, f32[16,2,512]{2,1,0:T(2,128)S(1)}) custom-call(s32[8]{0:T(128)S(1)} %pad_add_fusion.1.info_ref, bf16[512,1152]{1,0:T(8,128)(2,1)S(1)} %copy-done.1, bf16[16,3,32,1024]{3,2,1,0:T(8,128)(2,1)S(1)} %all-to-all-done.1.got_ref), custom_call_target="tpu_custom_call" | custom-call | tf_op jit(solution)/shard_map/pallas_call | solution.py:106
  109.1 12.3 %all_to_all.16 = f32[16,2,512]{2,1,0:T(2,128)S(1)} all-to-all(f32[16,2,512]{2,1,0:T(2,128)S(1)} %get-tuple-element.8), channel_id=1, replica_groups=mesh['cluster'=8,'shard'=16] {'shard'}, dimensions={0} | all-to-all | bytes 131072 | tf_op jit(solution)/shard_map/all_to_all | solution.py:116
  121.4 4.2 %collective-permute-done.1 = f32[512]{0:T(512)S(1)} collective-permute-done((f32[512]{0:T(512)S(1)}, f32[512]{0:T(512)S(1)}, u32[]{:S(2)}, u32[]{:S(2)}) %collective-permute-start.1) | collective-permute-done | bytes 2080 | tf_op jit(solution)/shard_map/ppermute | solution.py:117
  125.6 0.6 maximum_select_fusion
  (14 shorter events, 0.2 us)
Async XLA Ops:
  32.1 14.8 %collective-permute-start = (bf16[16,32,1152]{2,1,0:T(8,128)(2,1)S(1)}, bf16[16,32,1152]{2,1,0:T(8,128)(2,1)S(1)}, u32[]{:S(2)}, u32[]{:S(2)}) collective-permute-start(bf16[16,32,1152]{2,1,0:T(8,128)(2,1)S(1)} %all_to_all.15.own_ref), channel_id=1, source_target_pairs={{16,0},{32,16},{48,32},{64,48},{80,64},{96,80},{112,96},{0,112},{1... | collective-permute-start | bytes 3538952 | tf_op jit(solution)/shard_map/ppermute | solution.py:90
  46.8 1.9 %copy-start.2 = (bf16[16,32,1152]{2,1,0:T(8,128)(2,1)}, bf16[16,32,1152]{2,1,0:T(8,128)(2,1)S(1)}, u32[]{:S(2)}) copy-start(bf16[16,32,1152]{2,1,0:T(8,128)(2,1)S(1)} %collective-permute-done.next_ref) | copy-start | bytes 3538948
  48.7 1.6 %copy-start = (bf16[16,3,32,1024]{3,2,1,0:T(8,128)(2,1)}, bf16[16,3,32,1024]{3,2,1,0:T(8,128)(2,1)S(1)}, u32[]{:S(2)}) copy-start(bf16[16,3,32,1024]{3,2,1,0:T(8,128)(2,1)S(1)} %shard_map.38) | copy-start | bytes 9437188
  50.3 3.9 %copy-start.3 = (s32[1,4]{1,0:T(1,128)S(1)}, s32[1,4]{1,0:T(1,128)}, u32[]{:S(2)}) copy-start(s32[1,4]{1,0:T(1,128)} %param.4) | copy-start | bytes 52
  50.3 54.1 %all-to-all-start.1 = ((bf16[16,3,32,1024]{3,2,1,0:T(8,128)(2,1)}), bf16[16,3,32,1024]{3,2,1,0:T(8,128)(2,1)S(1)}, u32[]{:S(2)}, u32[]{:S(2)}) async-start(bf16[16,3,32,1024]{3,2,1,0:T(8,128)(2,1)} %copy-done), calls=%async_computation.1 | async-start | bytes 6291456 | tf_op jit(solution)/shard_map/all_to_all | solution.py:101
  104.5 1.3 %copy-start.1 = (bf16[512,1152]{1,0:T(8,128)(2,1)S(1)}, bf16[512,1152]{1,0:T(8,128)(2,1)}, u32[]{:S(2)}) copy-start(bf16[512,1152]{1,0:T(8,128)(2,1)} %shard_map.37.unit_ref) | copy-start | bytes 3538948
  121.4 4.2 %collective-permute-start.1 = (f32[512]{0:T(512)S(1)}, f32[512]{0:T(512)S(1)}, u32[]{:S(2)}, u32[]{:S(2)}) collective-permute-start(f32[512]{0:T(512)S(1)} %bitcast.24), channel_id=1, source_target_pairs={{0,16},{16,32},{32,48},{48,64},{64,80},{80,96},{96,112},{112,0},{1... | collective-permute-start | bytes 6152 | tf_op jit(solution)/shard_map/ppermute | solution.py:117

commit v2 on v1

v2 whole, which is shorter than its diff:
```python
import jax
import jax.numpy as jnp
from jax import lax
from jax.experimental import pallas as pl
from jax.experimental.pallas import tpu as pltpu
from jax.sharding import PartitionSpec as P

ROWS = 512
D = 1024
PAIRS = 4
SLOTS = PAIRS - 1
GROUP = 16
CUT = ROWS // GROUP
WIDE = D + 128
ENTRY = 8
STEP = 256
VMEM = pl.BlockSpec(memory_space=pltpu.VMEM)
SMEM = pl.BlockSpec(memory_space=pltpu.SMEM)


def normalise(partners_ref, counts_ref, doc_ref, out_ref):
    raw = doc_ref[...].astype(jnp.float32)
    inv = lax.rsqrt(jnp.sum(raw * raw, axis=1, keepdims=True) + 1e-06)
    out_ref[:, :D] = (raw * inv).astype(jnp.bfloat16)
    lane = lax.broadcasted_iota(jnp.int32, (STEP, WIDE - D), 1)
    entry = jnp.where(lane == 0, partners_ref[0, 0], 0)
    for p in range(1, PAIRS):
        entry = jnp.where(lane == p, partners_ref[0, p], entry)
    entry = jnp.where(lane == PAIRS, counts_ref[0] // 32, entry)
    entry = jnp.where(lane == PAIRS + 1, counts_ref[0] % 32, entry)
    out_ref[:, D:] = entry.astype(jnp.float32).astype(jnp.bfloat16)


def pick(table_ref, odd_ref, own_ref, near_ref, far_ref, out_ref):
    def one(e, carry):
        dst, slot = e // SLOTS, e % SLOTS
        code = table_ref[dst * ENTRY + 1 + slot]

        @pl.when(code < GROUP)
        def _():
            out_ref[dst, slot] = own_ref[code, :, :D]

        @pl.when(jnp.logical_and(code >= GROUP, odd_ref[0] == 0))
        def _():
            out_ref[dst, slot] = near_ref[code - GROUP, :, :D]

        @pl.when(jnp.logical_and(code >= GROUP, odd_ref[0] == 1))
        def _():
            out_ref[dst, slot] = far_ref[code - GROUP, :, :D]

        return carry

    lax.fori_loop(0, GROUP * SLOTS, one, 0)


def products(left, right):
    return lax.dot_general(left, right, (((1,), (1,)), ((), ())), preferred_element_type=jnp.float32)


def numbers():
    row = lax.broadcasted_iota(jnp.int32, (ROWS, 1), 0)
    col = lax.broadcasted_iota(jnp.int32, (1, ROWS), 1)
    return row, col


def folded(part, rows):
    for t in range(ROWS // 128):
        part = jnp.maximum(part, rows[:, t * 128 : (t + 1) * 128])
    return part


def self_scores(counts_ref, unit_ref, best_ref):
    unit = unit_ref[:, :D]
    row, col = numbers()
    keep = jnp.logical_and(col < counts_ref[0], row != col)
    rows = jnp.where(keep, products(unit, unit), -1.0)
    best_ref[...] = jnp.max(folded(jnp.full((ROWS, 128), -1.0, jnp.float32), rows).T, axis=0, keepdims=True)


def pair_scores(place_ref, partners_ref, counts_ref, own_table_ref, next_table_ref, unit_ref, got_ref, best_ref, send_ref, over_ref):
    odd, mine = place_ref[0], place_ref[1]
    unit = unit_ref[:, :D]
    row, col = numbers()
    row_ok = row < counts_ref[0]
    send_ref[...] = jnp.full(send_ref.shape, -1.0, jnp.float32)
    over_ref[...] = jnp.full(over_ref.shape, -1.0, jnp.float32)
    part = jnp.full((ROWS, 128), -1.0, jnp.float32)
    for p in range(SLOTS):
        code = partners_ref[0, 1 + p]
        at = (code % GROUP) * ENTRY + PAIRS
        own_count = own_table_ref[at] * 32 + own_table_ref[at + 1]
        next_count = next_table_ref[at] * 32 + next_table_ref[at + 1]
        other_count = jnp.where(code < GROUP, own_count, next_count)
        scores = products(unit, got_ref[:, p].reshape(ROWS, D))
        off = jnp.where(code == mine, 0, ROWS)
        scores = jnp.where(row + off == col, -1.0, scores)
        part = folded(part, jnp.where(col < other_count, scores, -1.0))
        cols = jnp.max(jnp.where(row_ok, scores, -1.0), axis=0, keepdims=True)
        line = code + jnp.where(odd == 1, 0, GROUP)

        @pl.when(line < 2 * GROUP)
        def _():
            send_ref[line] = jnp.maximum(send_ref[line], cols)

        @pl.when(line >= 2 * GROUP)
        def _():
            over_ref[line - 2 * GROUP] = jnp.maximum(over_ref[line - 2 * GROUP], cols)

    best_ref[...] = jnp.max(part.T, axis=0, keepdims=True)


def table_of(slices):
    return slices[:, 0, D : D + ENTRY].astype(jnp.int32).reshape(-1)


def shards(documents, partners, counts):
    n_cluster = lax.axis_size("cluster")
    my_cluster, my_shard = lax.axis_index("cluster"), lax.axis_index("shard")
    odd = my_cluster % 2
    unit = pl.pallas_call(
        normalise,
        grid=(ROWS // STEP,),
        in_specs=[SMEM, SMEM, pl.BlockSpec((STEP, D), lambda i: (i, 0))],
        out_specs=pl.BlockSpec((STEP, WIDE), lambda i: (i, 0)),
        out_shape=jax.ShapeDtypeStruct((ROWS, WIDE), jnp.bfloat16),
    )(partners, counts, documents)
    own = lax.all_to_all(unit.reshape(GROUP, CUT, WIDE), "shard", 0, 0, tiled=True)
    near = lax.ppermute(own, "cluster", [(c, c ^ 1) for c in range(n_cluster)])
    far = lax.ppermute(near, "cluster", [((c + 2) % n_cluster, c) for c in range(1, n_cluster, 2)])
    self_best = pl.pallas_call(
        self_scores,
        in_specs=[SMEM, VMEM],
        out_specs=VMEM,
        out_shape=jax.ShapeDtypeStruct((1, ROWS), jnp.float32),
        cost_estimate=pl.CostEstimate(flops=2 * ROWS * ROWS * D, bytes_accessed=ROWS * WIDE * 2, transcendentals=0),
    )(counts, unit)
    own_table = table_of(own)
    next_table = jnp.where(odd == 1, table_of(far), table_of(near))
    picked = pl.pallas_call(
        pick,
        in_specs=[SMEM, SMEM, VMEM, VMEM, VMEM],
        out_specs=VMEM,
        out_shape=jax.ShapeDtypeStruct((GROUP, SLOTS, CUT, D), jnp.bfloat16),
        compiler_params=pltpu.CompilerParams(vmem_limit_bytes=16 * 2**20),
    )(own_table, odd[None], own, near, far)
    got = lax.all_to_all(picked, "shard", 0, 0, tiled=True)
    best, send, over = pl.pallas_call(
        pair_scores,
        in_specs=[SMEM] * 5 + [VMEM] * 2,
        out_specs=[VMEM] * 3,
        out_shape=[
            jax.ShapeDtypeStruct((1, ROWS), jnp.float32),
            jax.ShapeDtypeStruct((2 * GROUP, 1, ROWS), jnp.float32),
            jax.ShapeDtypeStruct((GROUP, 1, ROWS), jnp.float32),
        ],
        compiler_params=pltpu.CompilerParams(vmem_limit_bytes=12 * 2**20),
    )(jnp.stack([odd, my_shard]), partners, counts, own_table, next_table, unit, got)
    over = lax.ppermute(over, "cluster", [(c, c + 1) for c in range(0, n_cluster, 2)])
    first = jnp.where(odd == 1, jnp.maximum(send[:GROUP], over), send[:GROUP])
    send = jnp.concatenate([first, send[GROUP:]])
    reach = [
        [c * GROUP + s for c in (odd_one, (odd_one + 1) % n_cluster) for s in range(GROUP)]
        for odd_one in range(1, n_cluster, 2)
    ]
    back = lax.all_to_all(send, ("cluster", "shard"), 0, 0, axis_index_groups=reach, tiled=True)
    best = jnp.maximum(jnp.maximum(best[0], self_best[0]), jnp.max(back, axis=(0, 1)))
    return jnp.where(jnp.arange(ROWS, dtype=jnp.int32) < counts[0], best, 0.0)


def solution(mesh):
    return jax.shard_map(
        shards,
        mesh=mesh,
        in_specs=(
            P(("cluster", "shard"), None),
            P(("cluster", "shard"), None),
            P(("cluster", "shard")),
        ),
        out_specs=P(("cluster", "shard")),
        check_vma=False,
    )
```

time: 127 us -> 112 us (0.88)
  waiting for transfers between devices: 66.1 us -> 38.9 us
  starting transfers between devices: 4.93 us -> 28.4 us
  blocking collectives: 38.8 us -> 26.5 us
  Pallas kernels: 8.79 us -> 11.1 us
  local copies, waits for them, and re-layouts: 4.46 us -> 3.1 us
    all_to_all x1, waiting for transfers between devices: 48.4 us -> 31.4 us  [shards(): got = lax.all_to_all(picked, 'shard', 0, 0, tiled=True)]
    ppermute x2 -> x3, starting transfers between devices: 1.05 us -> 16.1 us  [the longest x1 15.4 us: shards(): lax.ppermute(over, 'cluster', [(c, c + 1) for c in range(0, n_cluster, 2)])]
    ppermute x2 -> x3, waiting for transfers between devices: 17.7 us -> 3.69 us  [the longest x1 2.84 us: shards(): near = lax.ppermute(own, 'cluster', [(c, c ^ 1) for c in range(n_cluster)])]
    all_to_all x1 -> x0, blocking collectives: 12.3 us -> none  [shards(): back = jnp.max(lax.all_to_all(send, 'shard', 0, 0, tiled=True), axis=0)]
    all_to_all x0 -> x1, starting transfers between devices: none -> 8.39 us  [shards(): lax.all_to_all(send, ('cluster', 'shard'), 0, 0, axis_index_groups=reach,...]
    all_to_all x0 -> x1, waiting for transfers between devices: none -> 3.82 us  [shards(): lax.all_to_all(send, ('cluster', 'shard'), 0, 0, axis_index_groups=reach,...]
    pallas_call x3 -> x4, Pallas kernels: 8.79 us -> 11.1 us  [the longest x1 3.32 us: shards(): pl.pallas_call(pair_scores, in_specs=[SMEM] * 5 + [VMEM] * 2, out_specs=[...]
    convert_element_type x3 -> x1, other arithmetic: 1.51 us -> 0.03 us  [table_of(): return slices[:, 0, D:D + ENTRY].astype(jnp.int32).reshape(-1)]
  transfers between devices with their start and end apart: 3 -> 5, of which waited for: 3 -> 4; matrix products, arithmetic and copies ran while one was open for 2% -> 2% of each run, Pallas kernels for 0% -> 2%
where the time goes in v2:
time: 112 us
  waiting for transfers between devices  38.9 us (35%)
  starting transfers between devices  28.4 us (25%)
  blocking collectives  26.5 us (24%)
  Pallas kernels  11.1 us (10%)
  local copies, waits for them, and re-layouts  3.1 us (3%)
  other arithmetic  2.97 us (3%)
    all_to_all x1, waiting for transfers between devices, shards(): got = lax.all_to_all(picked, 'shard', 0, 0, tiled=True)  31.4 us
    all_to_all x1, blocking collectives, shards(): lax.all_to_all(unit.reshape(GROUP, CUT, WIDE), 'shard', 0, 0, tiled=True)  26.5 us
    ppermute x1, starting transfers between devices, shards(): lax.ppermute(over, 'cluster', [(c, c + 1) for c in range(0, n_cluster, 2)])  15.4 us
    all_to_all x1, starting transfers between devices, shards(): lax.all_to_all(send, ('cluster', 'shard'), 0, 0, axis_index_groups=reach,...  8.39 us
    all_to_all x1, starting transfers between devices, shards(): got = lax.all_to_all(picked, 'shard', 0, 0, tiled=True)  3.87 us
    all_to_all x1, waiting for transfers between devices, shards(): lax.all_to_all(send, ('cluster', 'shard'), 0, 0, axis_index_groups=reach,...  3.82 us
    pallas_call x1, Pallas kernels, shards(): pl.pallas_call(pair_scores, in_specs=[SMEM] * 5 + [VMEM] * 2, out_specs=[...  3.32 us
    unnamed x10, local copies, waits for them, and re-layouts  2.93 us
  transfers between devices with their start and end apart: 5, of which 4 were waited for; matrix products, arithmetic and copies ran while one was open for 2% of the time, Pallas kernels for 2%

profile of v2, /device:TPU:0, one launch (start us, length us, event | category | flops | bytes accessed | tf_op | source)
XLA Modules:
  0.0 111.8 jit_solution(2036222250606726520)
XLA Ops:
  0.7 2.3 %shard_map.37.unit_ref = bf16[512,1152]{1,0:T(8,128)(2,1)} custom-call(s32[1,4]{1,0:T(1,128)} %partners_ref.3, s32[1]{0:T(128)} %copy.4.counts_ref, bf16[512,1024]{1,0:T(8,128)(2,1)} %doc_ref.1), custom_call_target="tpu_custom_call" | custom-call | tf_op jit(solution)/shard_map/pallas_call | solution.py:120
  2.9 26.5 %all_to_all.15.own_ref = bf16[16,32,1152]{2,1,0:T(8,128)(2,1)S(1)} all-to-all(bf16[16,32,1152]{2,1,0:T(8,128)(2,1)} %bitcast.6), channel_id=1, replica_groups=mesh['cluster'=8,'shard'=16] {'shard'}, dimensions={0} | all-to-all | bytes 2359296 | tf_op jit(solution)/shard_map/all_to_all | solution.py:127
  29.5 0.0 collective-permute-start
  29.5 2.8 %collective-permute-done.near_ref = bf16[16,32,1152]{2,1,0:T(8,128)(2,1)S(1)} collective-permute-done((bf16[16,32,1152]{2,1,0:T(8,128)(2,1)S(1)}, bf16[16,32,1152]{2,1,0:T(8,128)(2,1)S(1)}, u32[]{:S(2)}, u32[]{:S(2)}) %collective-permute-start) | collective-permute-done | bytes 1179680 | tf_op jit(solution)/shard_map/ppermute | solution.py:128
  32.3 0.7 collective-permute-start.1
  33.1 0.1 reshape.17.table_ref.own_table_ref
  33.2 2.8 %shard_map.38 = bf16[16,3,32,1024]{3,2,1,0:T(8,128)(2,1)S(1)} custom-call(s32[128]{0:T(128)S(1)} %reshape.17.table_ref.own_table_ref, s32[1]{0:T(128)} %bitcast.1.odd_ref, bf16[16,32,1152]{2,1,0:T(8,128)(2,1)S(1)} %all_to_all.15.own_ref, bf16[16,32,1152]{2,1,0:T(8,128)(2,1)S(1)} %collective-permute-done.near_ref, ...), custom_call_target="tpu_custom_call" | custom-call | tf_op jit(solution)/shard_map/pallas_call | solution.py:139
  36.1 1.6 %copy-done = bf16[16,3,32,1024]{3,2,1,0:T(8,128)(2,1)} copy-done((bf16[16,3,32,1024]{3,2,1,0:T(8,128)(2,1)}, bf16[16,3,32,1024]{3,2,1,0:T(8,128)(2,1)S(1)}, u32[]{:S(2)}) %copy-start) | copy-done | bytes 3145752
  37.7 3.9 %all-to-all-start.1 = ((bf16[16,3,32,1024]{3,2,1,0:T(8,128)(2,1)}), bf16[16,3,32,1024]{3,2,1,0:T(8,128)(2,1)S(1)}, u32[]{:S(2)}, u32[]{:S(2)}) async-start(bf16[16,3,32,1024]{3,2,1,0:T(8,128)(2,1)} %copy-done), calls=%async_computation.1 | async-start | bytes 6291456 | tf_op jit(solution)/shard_map/all_to_all | solution.py:146
  41.6 0.1 pad_add_fusion.place_ref
  41.7 0.8 fusion
  42.5 0.1 select_n.32.next_table_ref
  42.6 31.4 %all-to-all-done.1.got_ref = bf16[16,3,32,1024]{3,2,1,0:T(8,128)(2,1)S(1)} async-done(((bf16[16,3,32,1024]{3,2,1,0:T(8,128)(2,1)}), bf16[16,3,32,1024]{3,2,1,0:T(8,128)(2,1)S(1)}, u32[]{:S(2)}, u32[]{:S(2)}) %all-to-all-start.1) | async-done | bytes 3145760 | tf_op jit(solution)/shard_map/all_to_all | solution.py:146
  74.0 1.3 %copy-done.1 = bf16[512,1152]{1,0:T(8,128)(2,1)S(1)} copy-done((bf16[512,1152]{1,0:T(8,128)(2,1)S(1)}, bf16[512,1152]{1,0:T(8,128)(2,1)}, u32[]{:S(2)}) %copy-start.1) | copy-done | bytes 1179672
  75.3 3.3 %shard_map.39 = (f32[1,512]{1,0:T(1,128)S(1)}, f32[32,1,512]{2,1,0:T(1,128)S(1)}, f32[16,1,512]{2,1,0:T(1,128)S(1)}) custom-call(s32[2]{0:T(128)S(1)} %pad_add_fusion.place_ref, s32[1,4]{1,0:T(1,128)S(1)} %copy-done.4, s32[1]{0:T(128)} %copy.4.counts_ref, s32[128]{0:T(128)S(1)} %reshape.17.table_ref.own_table_ref, s32[128]{0:T(128)S(1)} %select_n.32.next_table_ref, ...), custom_call_target="tpu_custom_call" | custom-call | tf_op jit(solution)/shard_map/pallas_call | solution.py:147
  78.6 15.4 %collective-permute-start.2 = (f32[16,1,512]{2,1,0:T(1,128)S(1)}, f32[16,1,512]{2,1,0:T(1,128)S(1)}, u32[]{:S(2)}, u32[]{:S(2)}) collective-permute-start(f32[16,1,512]{2,1,0:T(1,128)S(1)} %get-tuple-element.10), channel_id=1, source_target_pairs={{0,16},{32,48},{64,80},{96,112},{1,17},{33,49},{65,81},{97,113},{2... | collective-permute-start | bytes 98312 | tf_op jit(solution)/shard_map/ppermute | solution.py:158
  94.0 0.8 collective-permute-done.2
  94.9 0.7 pad_maximum_fusion
  95.6 8.4 %all-to-all-start.2 = ((f32[32,1,512]{2,1,0:T(1,128)}), f32[32,1,512]{2,1,0:T(1,128)S(1)}, u32[]{:S(2)}, u32[]{:S(2)}) async-start(f32[32,1,512]{2,1,0:T(1,128)} %pad_maximum_fusion), calls=%async_computation.2 | async-start | bytes 131072 | tf_op jit(solution)/shard_map/all_to_all | solution.py:165
  104.0 2.7 %shard_map.40 = f32[1,512]{1,0:T(1,128)} custom-call(s32[1]{0:T(128)} %copy.4.counts_ref, bf16[512,1152]{1,0:T(8,128)(2,1)} %shard_map.37.unit_ref), custom_call_target="tpu_custom_call" | custom-call | flops 536870912 | bytes 1179648 | tf_op jit(solution)/shard_map/pallas_call | solution.py:130
  106.7 0.7 max.12
  107.3 3.8 %all-to-all-done.2 = f32[32,1,512]{2,1,0:T(1,128)S(1)} async-done(((f32[32,1,512]{2,1,0:T(1,128)}), f32[32,1,512]{2,1,0:T(1,128)S(1)}, u32[]{:S(2)}, u32[]{:S(2)}) %all-to-all-start.2) | async-done | bytes 65568 | tf_op jit(solution)/shard_map/all_to_all | solution.py:165
  111.2 0.1 reduce_max.9
  111.2 0.6 maximum_select_fusion
  (11 shorter events, 0.1 us)
Async XLA Ops:
  29.5 2.8 %collective-permute-start = (bf16[16,32,1152]{2,1,0:T(8,128)(2,1)S(1)}, bf16[16,32,1152]{2,1,0:T(8,128)(2,1)S(1)}, u32[]{:S(2)}, u32[]{:S(2)}) collective-permute-start(bf16[16,32,1152]{2,1,0:T(8,128)(2,1)S(1)} %all_to_all.15.own_ref), channel_id=1, source_target_pairs={{0,16},{16,0},{32,48},{48,32},{64,80},{80,64},{96,112},{112,96},{1... | collective-permute-start | bytes 3538952 | tf_op jit(solution)/shard_map/ppermute | solution.py:128
  32.3 3.7 %copy-start.2 = (bf16[16,32,1152]{2,1,0:T(8,128)(2,1)}, bf16[16,32,1152]{2,1,0:T(8,128)(2,1)S(1)}, u32[]{:S(2)}) copy-start(bf16[16,32,1152]{2,1,0:T(8,128)(2,1)S(1)} %collective-permute-done.near_ref) | copy-start | bytes 3538948
  32.3 0.9 collective-permute-start.1
  33.2 2.9 %copy-start.3 = (bf16[16,32,1152]{2,1,0:T(8,128)(2,1)}, bf16[16,32,1152]{2,1,0:T(8,128)(2,1)S(1)}, u32[]{:S(2)}) copy-start(bf16[16,32,1152]{2,1,0:T(8,128)(2,1)S(1)} %collective-permute-done.1.far_ref) | copy-start | bytes 3538948
  36.0 1.7 %copy-start = (bf16[16,3,32,1024]{3,2,1,0:T(8,128)(2,1)}, bf16[16,3,32,1024]{3,2,1,0:T(8,128)(2,1)S(1)}, u32[]{:S(2)}) copy-start(bf16[16,3,32,1024]{3,2,1,0:T(8,128)(2,1)S(1)} %shard_map.38) | copy-start | bytes 9437188
  37.7 36.3 %copy-start.4 = (s32[1,4]{1,0:T(1,128)S(1)}, s32[1,4]{1,0:T(1,128)}, u32[]{:S(2)}) copy-start(s32[1,4]{1,0:T(1,128)} %partners_ref.3) | copy-start | bytes 52
  37.7 36.3 %all-to-all-start.1 = ((bf16[16,3,32,1024]{3,2,1,0:T(8,128)(2,1)}), bf16[16,3,32,1024]{3,2,1,0:T(8,128)(2,1)S(1)}, u32[]{:S(2)}, u32[]{:S(2)}) async-start(bf16[16,3,32,1024]{3,2,1,0:T(8,128)(2,1)} %copy-done), calls=%async_computation.1 | async-start | bytes 6291456 | tf_op jit(solution)/shard_map/all_to_all | solution.py:146
  74.0 1.3 %copy-start.1 = (bf16[512,1152]{1,0:T(8,128)(2,1)S(1)}, bf16[512,1152]{1,0:T(8,128)(2,1)}, u32[]{:S(2)}) copy-start(bf16[512,1152]{1,0:T(8,128)(2,1)} %shard_map.37.unit_ref) | copy-start | bytes 3538948
  78.6 16.3 %collective-permute-start.2 = (f32[16,1,512]{2,1,0:T(1,128)S(1)}, f32[16,1,512]{2,1,0:T(1,128)S(1)}, u32[]{:S(2)}, u32[]{:S(2)}) collective-permute-start(f32[16,1,512]{2,1,0:T(1,128)S(1)} %get-tuple-element.10), channel_id=1, source_target_pairs={{0,16},{32,48},{64,80},{96,112},{1,17},{33,49},{65,81},{97,113},{2... | collective-permute-start | bytes 98312 | tf_op jit(solution)/shard_map/ppermute | solution.py:158
  95.6 15.6 %all-to-all-start.2 = ((f32[32,1,512]{2,1,0:T(1,128)}), f32[32,1,512]{2,1,0:T(1,128)S(1)}, u32[]{:S(2)}, u32[]{:S(2)}) async-start(f32[32,1,512]{2,1,0:T(1,128)} %pad_maximum_fusion), calls=%async_computation.2 | async-start | bytes 131072 | tf_op jit(solution)/shard_map/all_to_all | solution.py:165

commit v3 on v2

--- a/solution.py
+++ b/solution.py
@@ -13,6 +13,7 @@
 CUT = ROWS // GROUP
 WIDE = D + 128
 ENTRY = 8
+HEAD = 8
 STEP = 256
 VMEM = pl.BlockSpec(memory_space=pltpu.VMEM)
 SMEM = pl.BlockSpec(memory_space=pltpu.SMEM)
@@ -77,20 +78,18 @@
     best_ref[...] = jnp.max(folded(jnp.full((ROWS, 128), -1.0, jnp.float32), rows).T, axis=0, keepdims=True)
 
 
-def pair_scores(place_ref, partners_ref, counts_ref, own_table_ref, next_table_ref, unit_ref, got_ref, best_ref, send_ref, over_ref):
-    odd, mine = place_ref[0], place_ref[1]
+def pair_scores(info_ref, unit_ref, got_ref, best_ref, send_ref, over_ref):
+    odd, mine = info_ref[0], info_ref[1]
     unit = unit_ref[:, :D]
     row, col = numbers()
-    row_ok = row < counts_ref[0]
+    row_ok = row < info_ref[2 + PAIRS]
     send_ref[...] = jnp.full(send_ref.shape, -1.0, jnp.float32)
     over_ref[...] = jnp.full(over_ref.shape, -1.0, jnp.float32)
     part = jnp.full((ROWS, 128), -1.0, jnp.float32)
     for p in range(SLOTS):
-        code = partners_ref[0, 1 + p]
-        at = (code % GROUP) * ENTRY + PAIRS
-        own_count = own_table_ref[at] * 32 + own_table_ref[at + 1]
-        next_count = next_table_ref[at] * 32 + next_table_ref[at + 1]
-        other_count = jnp.where(code < GROUP, own_count, next_count)
+        code = info_ref[3 + p]
+        at = HEAD + code * ENTRY + PAIRS
+        other_count = info_ref[at] * 32 + info_ref[at + 1]
         scores = products(unit, got_ref[:, p].reshape(ROWS, D))
         off = jnp.where(code == mine, 0, ROWS)
         scores = jnp.where(row + off == col, -1.0, scores)
@@ -127,13 +126,6 @@
     own = lax.all_to_all(unit.reshape(GROUP, CUT, WIDE), "shard", 0, 0, tiled=True)
     near = lax.ppermute(own, "cluster", [(c, c ^ 1) for c in range(n_cluster)])
     far = lax.ppermute(near, "cluster", [((c + 2) % n_cluster, c) for c in range(1, n_cluster, 2)])
-    self_best = pl.pallas_call(
-        self_scores,
-        in_specs=[SMEM, VMEM],
-        out_specs=VMEM,
-        out_shape=jax.ShapeDtypeStruct((1, ROWS), jnp.float32),
-        cost_estimate=pl.CostEstimate(flops=2 * ROWS * ROWS * D, bytes_accessed=ROWS * WIDE * 2, transcendentals=0),
-    )(counts, unit)
     own_table = table_of(own)
     next_table = jnp.where(odd == 1, table_of(far), table_of(near))
     picked = pl.pallas_call(
@@ -143,10 +135,12 @@
         out_shape=jax.ShapeDtypeStruct((GROUP, SLOTS, CUT, D), jnp.bfloat16),
         compiler_params=pltpu.CompilerParams(vmem_limit_bytes=16 * 2**20),
     )(own_table, odd[None], own, near, far)
+    head = jnp.concatenate([odd[None], my_shard[None], partners[0], counts, jnp.zeros((1,), jnp.int32)])
+    picked, info = lax.optimization_barrier((picked, jnp.concatenate([head, own_table, next_table])))
     got = lax.all_to_all(picked, "shard", 0, 0, tiled=True)
     best, send, over = pl.pallas_call(
         pair_scores,
-        in_specs=[SMEM] * 5 + [VMEM] * 2,
+        in_specs=[SMEM, VMEM, VMEM],
         out_specs=[VMEM] * 3,
         out_shape=[
             jax.ShapeDtypeStruct((1, ROWS), jnp.float32),
@@ -154,7 +148,15 @@
             jax.ShapeDtypeStruct((GROUP, 1, ROWS), jnp.float32),
         ],
         compiler_params=pltpu.CompilerParams(vmem_limit_bytes=12 * 2**20),
-    )(jnp.stack([odd, my_shard]), partners, counts, own_table, next_table, unit, got)
+    )(info, unit, got)
+    later, count, send, over, best = lax.optimization_barrier((unit, counts, send, over, best))
+    self_best = pl.pallas_call(
+        self_scores,
+        in_specs=[SMEM, VMEM],
+        out_specs=VMEM,
+        out_shape=jax.ShapeDtypeStruct((1, ROWS), jnp.float32),
+        cost_estimate=pl.CostEstimate(flops=2 * ROWS * ROWS * D, bytes_accessed=ROWS * WIDE * 2, transcendentals=0),
+    )(count, later)
     over = lax.ppermute(over, "cluster", [(c, c + 1) for c in range(0, n_cluster, 2)])
     first = jnp.where(odd == 1, jnp.maximum(send[:GROUP], over), send[:GROUP])
     send = jnp.concatenate([first, send[GROUP:]])

time: 112 us -> 103 us (0.920)
  waiting for transfers between devices: 38.9 us -> 7.53 us
  blocking collectives: 26.5 us -> 55.6 us
  starting transfers between devices: 28.4 us -> 24.7 us
  local copies, waits for them, and re-layouts: 3.1 us -> 0.91 us
    all_to_all x1 -> x0, waiting for transfers between devices: 31.4 us -> none  [shards(): got = lax.all_to_all(picked, 'shard', 0, 0, tiled=True)]
    all_to_all x0 -> x1, blocking collectives: none -> 29 us  [shards(): got = lax.all_to_all(picked, 'shard', 0, 0, tiled=True)]
    all_to_all x1 -> x0, starting transfers between devices: 3.87 us -> none  [shards(): got = lax.all_to_all(picked, 'shard', 0, 0, tiled=True)]
    unnamed x10 -> x2, local copies, waits for them, and re-layouts: 2.93 us -> 0.01 us
    ppermute x1, starting transfers between devices: 15.4 us -> 17.4 us  [shards(): lax.ppermute(over, 'cluster', [(c, c + 1) for c in range(0, n_cluster, 2)])]
    all_to_all x1, starting transfers between devices: 8.39 us -> 6.6 us  [shards(): lax.all_to_all(send, ('cluster', 'shard'), 0, 0, axis_index_groups=reach,...]
  transfers between devices with their start and end apart: 5 -> 4, of which waited for: 4 -> 3; matrix products, arithmetic and copies ran while one was open for 2% -> 1% of each run, Pallas kernels for 2% -> 3%
where the time goes in v3:
time: 103 us
  blocking collectives  55.6 us (54%)
  starting transfers between devices  24.7 us (24%)
  Pallas kernels  11.1 us (11%)
  waiting for transfers between devices  7.53 us (7%)
  other arithmetic  2.12 us (2%)
    all_to_all x1, blocking collectives, shards(): got = lax.all_to_all(picked, 'shard', 0, 0, tiled=True)  29 us
    all_to_all x1, blocking collectives, shards(): lax.all_to_all(unit.reshape(GROUP, CUT, WIDE), 'shard', 0, 0, tiled=True)  26.5 us
    ppermute x1, starting transfers between devices, shards(): lax.ppermute(over, 'cluster', [(c, c + 1) for c in range(0, n_cluster, 2)])  17.4 us
    all_to_all x1, starting transfers between devices, shards(): lax.all_to_all(send, ('cluster', 'shard'), 0, 0, axis_index_groups=reach,...  6.6 us
    all_to_all x1, waiting for transfers between devices, shards(): lax.all_to_all(send, ('cluster', 'shard'), 0, 0, axis_index_groups=reach,...  3.84 us
    pallas_call x1, Pallas kernels, shards(): pl.pallas_call(pair_scores, in_specs=[SMEM, VMEM, VMEM], out_specs=[VMEM]...  3.34 us
    ppermute x1, waiting for transfers between devices, shards(): near = lax.ppermute(own, 'cluster', [(c, c ^ 1) for c in range(n_cluster)])  2.84 us
    pallas_call x1, Pallas kernels, shards(): pl.pallas_call(pick, in_specs=[SMEM, SMEM, VMEM, VMEM, VMEM], out_specs=V...  2.82 us
  transfers between devices with their start and end apart: 4, of which 3 were waited for; matrix products, arithmetic and copies ran while one was open for 1% of the time, Pallas kernels for 3%

profile of v3, /device:TPU:0, one launch (start us, length us, event | category | flops | bytes accessed | tf_op | source)
XLA Modules:
  0.0 102.7 jit_solution(4396760172137189452)
XLA Ops:
  0.7 2.3 %shard_map.37.unit_ref = bf16[512,1152]{1,0:T(8,128)(2,1)} custom-call(s32[1,4]{1,0:T(1,128)} %partners_ref.1, s32[1]{0:T(128)} %copy.4.counts_ref, bf16[512,1024]{1,0:T(8,128)(2,1)} %doc_ref.1), custom_call_target="tpu_custom_call" | custom-call | tf_op jit(solution)/shard_map/pallas_call | solution.py:119
  2.9 26.5 %all_to_all.15.own_ref = bf16[16,32,1152]{2,1,0:T(8,128)(2,1)S(1)} all-to-all(bf16[16,32,1152]{2,1,0:T(8,128)(2,1)} %bitcast.7), channel_id=1, replica_groups=mesh['cluster'=8,'shard'=16] {'shard'}, dimensions={0} | all-to-all | bytes 2359296 | tf_op jit(solution)/shard_map/all_to_all | solution.py:126
  29.4 0.0 collective-permute-start
  29.4 2.8 %collective-permute-done.near_ref = bf16[16,32,1152]{2,1,0:T(8,128)(2,1)S(1)} collective-permute-done((bf16[16,32,1152]{2,1,0:T(8,128)(2,1)S(1)}, bf16[16,32,1152]{2,1,0:T(8,128)(2,1)S(1)}, u32[]{:S(2)}, u32[]{:S(2)}) %collective-permute-start) | collective-permute-done | bytes 1179680 | tf_op jit(solution)/shard_map/ppermute | solution.py:127
  32.3 0.7 collective-permute-start.1
  33.1 0.1 reshape.17.table_ref
  33.2 0.0 collective-permute-done.1.far_ref
  33.2 0.1 select_n.33
  33.3 0.7 concatenate.6.info_ref
  34.1 2.8 %shard_map.38 = bf16[16,3,32,1024]{3,2,1,0:T(8,128)(2,1)S(1)} custom-call(s32[128]{0:T(128)S(1)} %reshape.17.table_ref, s32[1]{0:T(128)} %bitcast.2.odd_ref, bf16[16,32,1152]{2,1,0:T(8,128)(2,1)S(1)} %all_to_all.15.own_ref, bf16[16,32,1152]{2,1,0:T(8,128)(2,1)S(1)} %collective-permute-done.near_ref, bf16[16,32,1152]{2,1,0:T(8,128)(2,1)S(1)} %collective-permute-done.1.far_ref), custom_call_target="tpu_custom_call" | custom-call | tf_op jit(solution)/shard_map/pallas_call | solution.py:131
  36.9 0.0 copy-start
  36.9 29.0 %all_to_all.16.got_ref = bf16[16,3,32,1024]{3,2,1,0:T(8,128)(2,1)S(1)} all-to-all(bf16[16,3,32,1024]{3,2,1,0:T(8,128)(2,1)S(1)} %shard_map.38), channel_id=1, replica_groups=mesh['cluster'=8,'shard'=16] {'shard'}, dimensions={0} | all-to-all | bytes 6291456 | tf_op jit(solution)/shard_map/all_to_all | solution.py:140
  65.9 0.0 copy-done
  65.9 3.3 %shard_map.39 = (f32[1,512]{1,0:T(1,128)S(1)}, f32[32,1,512]{2,1,0:T(1,128)S(1)}, f32[16,1,512]{2,1,0:T(1,128)S(1)}) custom-call(s32[264]{0:T(512)S(1)} %concatenate.6.info_ref, bf16[512,1152]{1,0:T(8,128)(2,1)S(1)} %copy-done, bf16[16,3,32,1024]{3,2,1,0:T(8,128)(2,1)S(1)} %all_to_all.16.got_ref), custom_call_target="tpu_custom_call" | custom-call | tf_op jit(solution)/shard_map/pallas_call | solution.py:141
  69.3 17.4 %collective-permute-start.2 = (f32[16,1,512]{2,1,0:T(1,128)S(1)}, f32[16,1,512]{2,1,0:T(1,128)S(1)}, u32[]{:S(2)}, u32[]{:S(2)}) collective-permute-start(f32[16,1,512]{2,1,0:T(1,128)S(1)} %get-tuple-element.24), channel_id=1, source_target_pairs={{0,16},{32,48},{64,80},{96,112},{1,17},{33,49},{65,81},{97,113},{2... | collective-permute-start | bytes 98312 | tf_op jit(solution)/shard_map/ppermute | solution.py:160
  86.6 0.8 collective-permute-done.2
  87.5 0.7 pad_maximum_fusion
  88.2 6.6 %all-to-all-start.2 = ((f32[32,1,512]{2,1,0:T(1,128)}), f32[32,1,512]{2,1,0:T(1,128)S(1)}, u32[]{:S(2)}, u32[]{:S(2)}) async-start(f32[32,1,512]{2,1,0:T(1,128)} %pad_maximum_fusion), calls=%async_computation.2 | async-start | bytes 131072 | tf_op jit(solution)/shard_map/all_to_all | solution.py:167
  94.8 2.7 %shard_map.40 = f32[1,512]{1,0:T(1,128)} custom-call(s32[1]{0:T(128)} %copy.4.counts_ref, bf16[512,1152]{1,0:T(8,128)(2,1)} %shard_map.37.unit_ref), custom_call_target="tpu_custom_call" | custom-call | flops 536870912 | bytes 1179648 | tf_op jit(solution)/shard_map/pallas_call | solution.py:153
  97.5 0.7 max.12
  98.2 3.8 %all-to-all-done.2 = f32[32,1,512]{2,1,0:T(1,128)S(1)} async-done(((f32[32,1,512]{2,1,0:T(1,128)}), f32[32,1,512]{2,1,0:T(1,128)S(1)}, u32[]{:S(2)}, u32[]{:S(2)}) %all-to-all-start.2) | async-done | bytes 65568 | tf_op jit(solution)/shard_map/all_to_all | solution.py:167
  102.0 0.1 reduce_max.9
  102.1 0.6 maximum_select_fusion
  (3 shorter events, 0.1 us)
Async XLA Ops:
  29.4 2.8 %collective-permute-start = (bf16[16,32,1152]{2,1,0:T(8,128)(2,1)S(1)}, bf16[16,32,1152]{2,1,0:T(8,128)(2,1)S(1)}, u32[]{:S(2)}, u32[]{:S(2)}) collective-permute-start(bf16[16,32,1152]{2,1,0:T(8,128)(2,1)S(1)} %all_to_all.15.own_ref), channel_id=1, source_target_pairs={{0,16},{16,0},{32,48},{48,32},{64,80},{80,64},{96,112},{112,96},{1... | collective-permute-start | bytes 3538952 | tf_op jit(solution)/shard_map/ppermute | solution.py:127
  32.3 0.9 collective-permute-start.1
  36.9 29.1 %copy-start = (bf16[512,1152]{1,0:T(8,128)(2,1)S(1)}, bf16[512,1152]{1,0:T(8,128)(2,1)}, u32[]{:S(2)}) copy-start(bf16[512,1152]{1,0:T(8,128)(2,1)} %shard_map.37.unit_ref) | copy-start | bytes 3538948
  69.3 18.2 %collective-permute-start.2 = (f32[16,1,512]{2,1,0:T(1,128)S(1)}, f32[16,1,512]{2,1,0:T(1,128)S(1)}, u32[]{:S(2)}, u32[]{:S(2)}) collective-permute-start(f32[16,1,512]{2,1,0:T(1,128)S(1)} %get-tuple-element.24), channel_id=1, source_target_pairs={{0,16},{32,48},{64,80},{96,112},{1,17},{33,49},{65,81},{97,113},{2... | collective-permute-start | bytes 98312 | tf_op jit(solution)/shard_map/ppermute | solution.py:160
  88.2 13.8 %all-to-all-start.2 = ((f32[32,1,512]{2,1,0:T(1,128)}), f32[32,1,512]{2,1,0:T(1,128)S(1)}, u32[]{:S(2)}, u32[]{:S(2)}) async-start(f32[32,1,512]{2,1,0:T(1,128)} %pad_maximum_fusion), calls=%async_computation.2 | async-start | bytes 131072 | tf_op jit(solution)/shard_map/all_to_all | solution.py:167

commit v4 on v3

v4 whole, which is shorter than its diff:
```python
import jax
import jax.numpy as jnp
from jax import lax
from jax.experimental import pallas as pl
from jax.experimental.pallas import tpu as pltpu
from jax.sharding import PartitionSpec as P

ROWS = 512
D = 1024
PAIRS = 4
SLOTS = PAIRS - 1
GROUP = 16
CUT = ROWS // GROUP
WIDE = D + 128
STEP = 128
VMEM = pl.BlockSpec(memory_space=pltpu.VMEM)
SMEM = pl.BlockSpec(memory_space=pltpu.SMEM)
ANY = pl.BlockSpec(memory_space=pl.ANY)


def unit_rows(raw):
    raw = raw.astype(jnp.float32)
    return raw * lax.rsqrt(jnp.sum(raw * raw, axis=1, keepdims=True) + 1e-06)


def normalise(partners_ref, counts_ref, doc_ref, out_ref, raw, unit, partners, counts, in_sem, out_sem, small_sem):
    small = [
        pltpu.make_async_copy(partners_ref, partners, small_sem.at[0]),
        pltpu.make_async_copy(counts_ref, counts, small_sem.at[1]),
    ]
    fetch = [
        pltpu.make_async_copy(doc_ref.at[pl.ds(i, STEP)], raw.at[pl.ds(i, STEP)], in_sem.at[i // STEP])
        for i in range(0, ROWS, STEP)
    ]
    store = [
        pltpu.make_async_copy(unit.at[pl.ds(i, STEP)], out_ref.at[pl.ds(i, STEP)], out_sem.at[i // STEP])
        for i in range(0, ROWS, STEP)
    ]
    for copy in small + fetch:
        copy.start()
    for copy in small:
        copy.wait()
    lane = lax.broadcasted_iota(jnp.int32, (16, WIDE - D), 1)
    entry = jnp.where(lane == 0, partners[0, 0], 0)
    for p in range(1, PAIRS):
        entry = jnp.where(lane == p, partners[0, p], entry)
    entry = entry.astype(jnp.float32).astype(jnp.bfloat16)
    for i in range(0, ROWS, STEP):
        fetch[i // STEP].wait()
        rows = unit_rows(raw[i : i + STEP])
        if i == 0:
            first = rows[:1]
        row = i + lax.broadcasted_iota(jnp.int32, (STEP, 1), 0)
        unit[i : i + STEP, :D] = jnp.where(row < counts[0], rows, first).astype(jnp.bfloat16)
        for j in range(i, i + STEP, 16):
            unit[j : j + 16, D:] = entry
        store[i // STEP].start()
    for copy in store:
        copy.wait()


def pick(table_ref, odd_ref, own_ref, near_ref, far_ref, out_ref):
    def all_from(next_ref):
        for e in range(GROUP * SLOTS):
            dst, slot = e // SLOTS, e % SLOTS
            code = table_ref[dst * PAIRS + 1 + slot]

            @pl.when(code < GROUP)
            def _():
                out_ref[dst, slot] = own_ref[code, :, :D]

            @pl.when(code >= GROUP)
            def _():
                out_ref[dst, slot] = next_ref[code - GROUP, :, :D]

    @pl.when(odd_ref[0] == 0)
    def _():
        all_from(near_ref)

    @pl.when(odd_ref[0] == 1)
    def _():
        all_from(far_ref)


def products(left, right):
    return lax.dot_general(left, right, (((1,), (1,)), ((), ())), preferred_element_type=jnp.float32)


def folded(part, rows):
    for t in range(rows.shape[1] // 128):
        part = jnp.maximum(part, rows[:, t * 128 : (t + 1) * 128])
    return part


def self_scores(counts_ref, unit_ref, best_ref):
    unit = unit_ref[:, :D]
    row = lax.broadcasted_iota(jnp.int32, (ROWS, 1), 0)
    col = lax.broadcasted_iota(jnp.int32, (1, ROWS), 1)
    keep = jnp.logical_and(col < counts_ref[0], row != col)
    rows = jnp.where(keep, products(unit, unit), -1.0)
    best_ref[...] = jnp.max(folded(jnp.full((ROWS, 128), -1.0, jnp.float32), rows).T, axis=0, keepdims=True)


def pair_scores(info_ref, unit_ref, got_ref, best_ref, send_ref, over_ref=None):
    odd, mine = info_ref[0], info_ref[1]
    unit = unit_ref[:, :D]
    send_ref[...] = jnp.full(send_ref.shape, -1.0, jnp.float32)
    part = jnp.full((ROWS, 128), -1.0, jnp.float32)
    for p in range(SLOTS):
        code = info_ref[3 + p]
        twice = code == mine
        scores = products(unit, got_ref[:, p].reshape(ROWS, D))
        part = jnp.where(twice, part, folded(part, scores))
        cols = jnp.where(twice, -1.0, jnp.max(scores, axis=0, keepdims=True))
        line = code + jnp.where(odd == 1, 0, GROUP)

        @pl.when(line < 2 * GROUP)
        def _():
            send_ref[line] = jnp.maximum(send_ref[line], cols)

        if over_ref is not None:

            @pl.when(line >= 2 * GROUP)
            def _():
                over_ref[line - 2 * GROUP] = jnp.maximum(over_ref[line - 2 * GROUP], cols)

    best_ref[...] = jnp.max(part.T, axis=0, keepdims=True)


def even_scores(info_ref, unit_ref, got_ref, best_ref, send_ref, over_ref):
    over_ref[...] = jnp.full(over_ref.shape, -1.0, jnp.float32)

    @pl.when(info_ref[0] == 0)
    def _():
        pair_scores(info_ref, unit_ref, got_ref, best_ref, send_ref, over_ref)


def odd_scores(info_ref, unit_ref, got_ref, held_best_ref, held_send_ref, best_ref, send_ref):
    @pl.when(info_ref[0] == 1)
    def _():
        pair_scores(info_ref, unit_ref, got_ref, best_ref, send_ref)

    @pl.when(info_ref[0] == 0)
    def _():
        best_ref[...] = held_best_ref[...]
        send_ref[...] = held_send_ref[...]


def shards(documents, partners, counts):
    n_cluster = lax.axis_size("cluster")
    my_cluster, my_shard = lax.axis_index("cluster"), lax.axis_index("shard")
    odd = my_cluster % 2
    unit = pl.pallas_call(
        normalise,
        in_specs=[ANY] * 3,
        out_specs=ANY,
        out_shape=jax.ShapeDtypeStruct((ROWS, WIDE), jnp.bfloat16),
        scratch_shapes=[
            pltpu.VMEM((ROWS, D), jnp.bfloat16),
            pltpu.VMEM((ROWS, WIDE), jnp.bfloat16),
            pltpu.SMEM((1, PAIRS), jnp.int32),
            pltpu.SMEM((1,), jnp.int32),
            pltpu.SemaphoreType.DMA((ROWS // STEP,)),
            pltpu.SemaphoreType.DMA((ROWS // STEP,)),
            pltpu.SemaphoreType.DMA((2,)),
        ],
    )(partners, counts, documents)
    own = lax.all_to_all(unit.reshape(GROUP, CUT, WIDE), "shard", 0, 0, tiled=True)
    near = lax.ppermute(own, "cluster", [(c, c ^ 1) for c in range(n_cluster)])
    far = lax.ppermute(near, "cluster", [((c + 2) % n_cluster, c) for c in range(1, n_cluster, 2)])
    table = own[:, 0, D : D + PAIRS].astype(jnp.int32).reshape(-1)
    picked = pl.pallas_call(
        pick,
        in_specs=[SMEM, SMEM, VMEM, VMEM, VMEM],
        out_specs=VMEM,
        out_shape=jax.ShapeDtypeStruct((GROUP, SLOTS, CUT, D), jnp.bfloat16),
        compiler_params=pltpu.CompilerParams(vmem_limit_bytes=16 * 2**20),
    )(table, odd[None], own, near, far)
    info = jnp.concatenate([odd[None], my_shard[None], partners[0]])
    picked, info, is_odd = lax.optimization_barrier((picked, info, odd == 1))
    got = lax.all_to_all(picked, "shard", 0, 0, tiled=True)
    best_shape = jax.ShapeDtypeStruct((1, ROWS), jnp.float32)
    send_shape = jax.ShapeDtypeStruct((2 * GROUP, 1, ROWS), jnp.float32)
    over_shape = jax.ShapeDtypeStruct((GROUP, 1, ROWS), jnp.float32)
    params = pltpu.CompilerParams(vmem_limit_bytes=12 * 2**20)
    best, send, over = pl.pallas_call(
        even_scores,
        in_specs=[SMEM, VMEM, VMEM],
        out_specs=[VMEM] * 3,
        out_shape=[best_shape, send_shape, over_shape],
        compiler_params=params,
    )(info, unit, got)
    over = lax.ppermute(over, "cluster", [(c, c + 1) for c in range(0, n_cluster, 2)])
    best, send = pl.pallas_call(
        odd_scores,
        in_specs=[SMEM] + [VMEM] * 4,
        out_specs=[VMEM] * 2,
        out_shape=[best_shape, send_shape],
        input_output_aliases={3: 0, 4: 1},
        compiler_params=params,
        cost_estimate=pl.CostEstimate(flops=SLOTS * 2 * ROWS * ROWS * D, bytes_accessed=4 * ROWS * D * 2, transcendentals=0),
    )(info, unit, got, best, send)
    later, count, send, best = lax.optimization_barrier((unit, counts, send, best))
    self_best = pl.pallas_call(
        self_scores,
        in_specs=[SMEM, VMEM],
        out_specs=VMEM,
        out_shape=jax.ShapeDtypeStruct((1, ROWS), jnp.float32),
        cost_estimate=pl.CostEstimate(flops=2 * ROWS * ROWS * D, bytes_accessed=ROWS * WIDE * 2, transcendentals=0),
    )(count, later)
    first = jnp.where(is_odd, jnp.maximum(send[:GROUP], over), send[:GROUP])
    send = jnp.concatenate([first, send[GROUP:]])
    reach = [
        [c * GROUP + s for c in (odd_one, (odd_one + 1) % n_cluster) for s in range(GROUP)]
        for odd_one in range(1, n_cluster, 2)
    ]
    back = lax.all_to_all(send, ("cluster", "shard"), 0, 0, axis_index_groups=reach, tiled=True)
    best = jnp.maximum(jnp.maximum(best[0], self_best[0]), jnp.max(back, axis=(0, 1)))
    return jnp.where(jnp.arange(ROWS, dtype=jnp.int32) < counts[0], best, 0.0)


def solution(mesh):
    return jax.shard_map(
        shards,
        mesh=mesh,
        in_specs=(
            P(("cluster", "shard"), None),
            P(("cluster", "shard"), None),
            P(("cluster", "shard")),
        ),
        out_specs=P(("cluster", "shard")),
        check_vma=False,
    )
```

time: 103 us -> 99.3 us (0.964)
  starting transfers between devices: 24.7 us -> 23.5 us
  Pallas kernels: 11.1 us -> 9.91 us
    ppermute x1, starting transfers between devices: 17.4 us -> 15 us  [shards(): lax.ppermute(over, 'cluster', [(c, c + 1) for c in range(0, n_cluster, 2)])]
    pallas_call x1, Pallas kernels: 2.82 us -> 1.32 us  [shards(): pl.pallas_call(pick, in_specs=[SMEM, SMEM, VMEM, VMEM, VMEM], out_specs=V...]
    all_to_all x1, starting transfers between devices: 6.6 us -> 7.76 us  [shards(): lax.all_to_all(send, ('cluster', 'shard'), 0, 0, axis_index_groups=reach,...]
    pallas_call x2 -> x3, Pallas kernels: 5.61 us -> 5.91 us  [the longest x1 2.96 us: shards(): pl.pallas_call(even_scores, in_specs=[SMEM, VMEM, VMEM], out_specs=[VMEM]...]
where the time goes in v4:
time: 99.3 us; the launch traced here: 98.9 us
  blocking collectives  55.6 us (56%)
  starting transfers between devices  23.5 us (24%)
  Pallas kernels  9.91 us (10%)
  waiting for transfers between devices  6.95 us (7%)
  other arithmetic  2.16 us (2%)
    all_to_all x1, blocking collectives, shards(): got = lax.all_to_all(picked, 'shard', 0, 0, tiled=True)  29 us
    all_to_all x1, blocking collectives, shards(): lax.all_to_all(unit.reshape(GROUP, CUT, WIDE), 'shard', 0, 0, tiled=True)  26.5 us
    ppermute x1, starting transfers between devices, shards(): lax.ppermute(over, 'cluster', [(c, c + 1) for c in range(0, n_cluster, 2)])  15 us
    all_to_all x1, starting transfers between devices, shards(): lax.all_to_all(send, ('cluster', 'shard'), 0, 0, axis_index_groups=reach,...  7.76 us
    all_to_all x1, waiting for transfers between devices, shards(): lax.all_to_all(send, ('cluster', 'shard'), 0, 0, axis_index_groups=reach,...  3.85 us
    pallas_call x1, Pallas kernels, shards(): pl.pallas_call(even_scores, in_specs=[SMEM, VMEM, VMEM], out_specs=[VMEM]...  2.96 us
    ppermute x1, waiting for transfers between devices, shards(): near = lax.ppermute(own, 'cluster', [(c, c ^ 1) for c in range(n_cluster)])  2.84 us
    pallas_call x1, Pallas kernels, shards(): pl.pallas_call(self_scores, in_specs=[SMEM, VMEM], out_specs=VMEM, out_sh...  2.67 us
  transfers between devices with their start and end apart: 4, of which 3 were waited for; matrix products, arithmetic and copies ran while one was open for 1% of the time, Pallas kernels for 3%

profile of v4, /device:TPU:0, one launch (start us, length us, event | category | flops | bytes accessed | tf_op | source)
XLA Modules:
  0.0 98.9 jit_solution(3717109083098245368)
XLA Ops:
  0.7 2.4 %shard_map.37.unit_ref = bf16[512,1152]{1,0:T(8,128)(2,1)} custom-call(s32[1,4]{1,0:T(1,128)} %partners_ref.1, s32[1]{0:T(128)} %copy.8.counts_ref, bf16[512,1024]{1,0:T(8,128)(2,1)} %doc_ref.1), custom_call_target="tpu_custom_call" | custom-call | tf_op jit(solution)/shard_map/pallas_call | solution.py:153
  3.0 0.0 copy-start.1
  3.0 26.5 %all_to_all.15.own_ref = bf16[16,32,1152]{2,1,0:T(8,128)(2,1)S(1)} all-to-all(bf16[16,32,1152]{2,1,0:T(8,128)(2,1)} %bitcast.7), channel_id=1, replica_groups=mesh['cluster'=8,'shard'=16] {'shard'}, dimensions={0} | all-to-all | bytes 2359296 | tf_op jit(solution)/shard_map/all_to_all | solution.py:168
  29.6 0.0 collective-permute-start
  29.6 2.8 %collective-permute-done.near_ref = bf16[16,32,1152]{2,1,0:T(8,128)(2,1)S(1)} collective-permute-done((bf16[16,32,1152]{2,1,0:T(8,128)(2,1)S(1)}, bf16[16,32,1152]{2,1,0:T(8,128)(2,1)S(1)}, u32[]{:S(2)}, u32[]{:S(2)}) %collective-permute-start) | collective-permute-done | bytes 1179680 | tf_op jit(solution)/shard_map/ppermute | solution.py:169
  32.4 0.7 collective-permute-start.1
  33.2 0.0 copy-done.1
  33.2 0.1 pad_add_fusion.info_ref
  33.3 0.1 reshape.9.table_ref
  33.4 0.0 collective-permute-done.1.far_ref
  33.4 1.3 %shard_map.38 = bf16[16,3,32,1024]{3,2,1,0:T(8,128)(2,1)S(1)} custom-call(s32[64]{0:T(128)S(1)} %reshape.9.table_ref, s32[1]{0:T(128)} %bitcast.2.odd_ref, bf16[16,32,1152]{2,1,0:T(8,128)(2,1)S(1)} %all_to_all.15.own_ref, bf16[16,32,1152]{2,1,0:T(8,128)(2,1)S(1)} %collective-permute-done.near_ref, bf16[16,32,1152]{2,1,0:T(8,128)(2,1)S(1)} %collective-permute-done.1.far_ref), custom_call_target="tpu_custom_call" | custom-call | tf_op jit(solution)/shard_map/pallas_call | solution.py:172
  34.7 0.0 copy-start
  34.7 29.0 %all_to_all.16.got_ref = bf16[16,3,32,1024]{3,2,1,0:T(8,128)(2,1)S(1)} all-to-all(bf16[16,3,32,1024]{3,2,1,0:T(8,128)(2,1)S(1)} %shard_map.38), channel_id=1, replica_groups=mesh['cluster'=8,'shard'=16] {'shard'}, dimensions={0} | all-to-all | bytes 6291456 | tf_op jit(solution)/shard_map/all_to_all | solution.py:181
  63.8 3.0 %shard_map.39 = (f32[1,512]{1,0:T(1,128)S(1)}, f32[32,1,512]{2,1,0:T(1,128)S(1)}, f32[16,1,512]{2,1,0:T(1,128)S(1)}) custom-call(s32[6]{0:T(128)S(1)} %pad_add_fusion.info_ref, bf16[512,1152]{1,0:T(8,128)(2,1)S(1)} %copy-done, bf16[16,3,32,1024]{3,2,1,0:T(8,128)(2,1)S(1)} %all_to_all.16.got_ref), custom_call_target="tpu_custom_call" | custom-call | tf_op jit(solution)/shard_map/pallas_call | solution.py:186
  66.7 15.0 %collective-permute-start.2 = (f32[16,1,512]{2,1,0:T(1,128)S(1)}, f32[16,1,512]{2,1,0:T(1,128)S(1)}, u32[]{:S(2)}, u32[]{:S(2)}) collective-permute-start(f32[16,1,512]{2,1,0:T(1,128)S(1)} %get-tuple-element.28), channel_id=1, source_target_pairs={{0,16},{32,48},{64,80},{96,112},{1,17},{33,49},{65,81},{97,113},{2... | collective-permute-start | bytes 98312 | tf_op jit(solution)/shard_map/ppermute | solution.py:193
  81.7 0.6 shard_map.40
  82.3 0.3 collective-permute-done.2
  82.6 0.7 pad_maximum_fusion
  83.3 7.8 %all-to-all-start.2 = ((f32[32,1,512]{2,1,0:T(1,128)}), f32[32,1,512]{2,1,0:T(1,128)S(1)}, u32[]{:S(2)}, u32[]{:S(2)}) async-start(f32[32,1,512]{2,1,0:T(1,128)} %pad_maximum_fusion), calls=%async_computation.2 | async-start | bytes 131072 | tf_op jit(solution)/shard_map/all_to_all | solution.py:217
  91.0 2.7 %shard_map.41 = f32[1,512]{1,0:T(1,128)} custom-call(s32[1]{0:T(128)} %copy.8.counts_ref, bf16[512,1152]{1,0:T(8,128)(2,1)} %shard_map.37.unit_ref), custom_call_target="tpu_custom_call" | custom-call | flops 536870912 | bytes 1179648 | tf_op jit(solution)/shard_map/pallas_call | solution.py:204
  93.7 0.7 max.12
  94.4 3.8 %all-to-all-done.2 = f32[32,1,512]{2,1,0:T(1,128)S(1)} async-done(((f32[32,1,512]{2,1,0:T(1,128)}), f32[32,1,512]{2,1,0:T(1,128)S(1)}, u32[]{:S(2)}, u32[]{:S(2)}) %all-to-all-start.2) | async-done | bytes 65568 | tf_op jit(solution)/shard_map/all_to_all | solution.py:217
  98.2 0.1 reduce_max.9
  98.3 0.6 maximum_select_fusion
  (3 shorter events, 0.1 us)
Async XLA Ops:
  3.0 30.1 %copy-start.1 = (s32[1,4]{1,0:T(1,128)S(1)}, s32[1,4]{1,0:T(1,128)}, u32[]{:S(2)}) copy-start(s32[1,4]{1,0:T(1,128)} %partners_ref.1) | copy-start | bytes 52
  29.6 2.8 %collective-permute-start = (bf16[16,32,1152]{2,1,0:T(8,128)(2,1)S(1)}, bf16[16,32,1152]{2,1,0:T(8,128)(2,1)S(1)}, u32[]{:S(2)}, u32[]{:S(2)}) collective-permute-start(bf16[16,32,1152]{2,1,0:T(8,128)(2,1)S(1)} %all_to_all.15.own_ref), channel_id=1, source_target_pairs={{0,16},{16,0},{32,48},{48,32},{64,80},{80,64},{96,112},{112,96},{1... | collective-permute-start | bytes 3538952 | tf_op jit(solution)/shard_map/ppermute | solution.py:169
  32.4 1.0 collective-permute-start.1
  34.7 29.0 %copy-start = (bf16[512,1152]{1,0:T(8,128)(2,1)S(1)}, bf16[512,1152]{1,0:T(8,128)(2,1)}, u32[]{:S(2)}) copy-start(bf16[512,1152]{1,0:T(8,128)(2,1)} %shard_map.37.unit_ref) | copy-start | bytes 3538948
  66.7 15.8 %collective-permute-start.2 = (f32[16,1,512]{2,1,0:T(1,128)S(1)}, f32[16,1,512]{2,1,0:T(1,128)S(1)}, u32[]{:S(2)}, u32[]{:S(2)}) collective-permute-start(f32[16,1,512]{2,1,0:T(1,128)S(1)} %get-tuple-element.28), channel_id=1, source_target_pairs={{0,16},{32,48},{64,80},{96,112},{1,17},{33,49},{65,81},{97,113},{2... | collective-permute-start | bytes 98312 | tf_op jit(solution)/shard_map/ppermute | solution.py:193
  83.3 15.0 %all-to-all-start.2 = ((f32[32,1,512]{2,1,0:T(1,128)}), f32[32,1,512]{2,1,0:T(1,128)S(1)}, u32[]{:S(2)}, u32[]{:S(2)}) async-start(f32[32,1,512]{2,1,0:T(1,128)} %pad_maximum_fusion), calls=%async_computation.2 | async-start | bytes 131072 | tf_op jit(solution)/shard_map/all_to_all | solution.py:217

commit v5 on v4

v5 whole, which is shorter than its diff:
```python
import jax
import jax.numpy as jnp
from jax import lax
from jax.experimental import pallas as pl
from jax.experimental.pallas import tpu as pltpu
from jax.sharding import PartitionSpec as P

ROWS = 512
D = 1024
PAIRS = 4
SLOTS = PAIRS - 1
GROUP = 16
CUT = ROWS // GROUP
LANES = 128
TILES = D // LANES
BODY = TILES * CUT
TALL = BODY + 16
STEP = 128
ORDER = [10, 15, 13, 11, 2, 14, 6, 7, 0, 9, 5, 4, 8, 1, 3, 12]
REACH = ORDER
PLACE = [ORDER.index(s) for s in range(GROUP)]
REACH_PLACE = [REACH.index(s) for s in range(GROUP)]
VMEM = pl.BlockSpec(memory_space=pltpu.VMEM)
SMEM = pl.BlockSpec(memory_space=pltpu.SMEM)
ANY = pl.BlockSpec(memory_space=pl.ANY)


def moved(code, places):
    shard = code % GROUP
    place = shard
    for s in range(GROUP):
        place = jnp.where(shard == s, places[s], place)
    return place + code - shard


def by_place(code):
    return moved(code, PLACE)


def to_reach(code):
    return moved(code, REACH_PLACE)


def unit_rows(raw):
    raw = raw.astype(jnp.float32)
    return raw * lax.rsqrt(jnp.sum(raw * raw, axis=1, keepdims=True) + 1e-06)


def normalise(partners_ref, counts_ref, doc_ref, out_ref, raw, unit, partners, counts, in_sem, out_sem, small_sem):
    small = [
        pltpu.make_async_copy(partners_ref, partners, small_sem.at[0]),
        pltpu.make_async_copy(counts_ref, counts, small_sem.at[1]),
    ]
    fetch = [
        pltpu.make_async_copy(doc_ref.at[pl.ds(i, STEP)], raw.at[pl.ds(i, STEP)], in_sem.at[i // STEP])
        for i in range(0, ROWS, STEP)
    ]
    store = [
        pltpu.make_async_copy(unit.at[pl.ds(i, STEP // CUT)], out_ref.at[pl.ds(i, STEP // CUT)], out_sem.at[i * CUT // STEP])
        for i in range(0, GROUP, STEP // CUT)
    ]
    for copy in small + fetch:
        copy.start()
    for copy in small:
        copy.wait()
    lane = lax.broadcasted_iota(jnp.int32, (16, LANES), 1)
    entry = jnp.where(lane == 0, by_place(partners[0, 0]), 0)
    for p in range(1, PAIRS):
        entry = jnp.where(lane == p, by_place(partners[0, p]), entry)
    entry = entry.astype(jnp.float32).astype(jnp.bfloat16)
    for i in range(0, ROWS, STEP):
        fetch[i // STEP].wait()
        rows = unit_rows(raw[i : i + STEP])
        if i == 0:
            first = rows[:1]
        row = i + lax.broadcasted_iota(jnp.int32, (STEP, 1), 0)
        rows = jnp.where(row < counts[0], rows, first).astype(jnp.bfloat16)
        for j in range(0, STEP, CUT):
            at = (i + j) // CUT
            for t in range(TILES):
                unit[at, t * CUT : (t + 1) * CUT] = rows[j : j + CUT, t * LANES : (t + 1) * LANES]
            unit[at, BODY:] = entry
        store[i // STEP].start()
    for copy in store:
        copy.wait()


def pick(table_ref, odd_ref, own_ref, near_ref, far_ref, out_ref):
    def all_from(next_ref):
        for e in range(GROUP * SLOTS):
            dst, slot = e // SLOTS, e % SLOTS
            code = table_ref[dst * PAIRS + 1 + slot]

            @pl.when(code < GROUP)
            def _():
                out_ref[dst, slot] = own_ref[code, :BODY]

            @pl.when(code >= GROUP)
            def _():
                out_ref[dst, slot] = next_ref[code - GROUP, :BODY]

    @pl.when(odd_ref[0] == 0)
    def _():
        all_from(near_ref)

    @pl.when(odd_ref[0] == 1)
    def _():
        all_from(far_ref)


def rows_of(slices):
    tiles = [slices[:, t * CUT : (t + 1) * CUT].reshape(ROWS, LANES) for t in range(TILES)]
    return jnp.concatenate(tiles, axis=1)


def products(left, right):
    return lax.dot_general(left, right, (((1,), (1,)), ((), ())), preferred_element_type=jnp.float32)


def folded(part, rows):
    for t in range(rows.shape[1] // 128):
        part = jnp.maximum(part, rows[:, t * 128 : (t + 1) * 128])
    return part


def self_part(count, unit):
    row = lax.broadcasted_iota(jnp.int32, (ROWS, 1), 0)
    col = lax.broadcasted_iota(jnp.int32, (1, ROWS), 1)
    rows = jnp.where(jnp.logical_and(col < count, row != col), products(unit, unit), -1.0)
    return folded(jnp.full((ROWS, 128), -1.0, jnp.float32), rows)


def highest(part):
    return jnp.max(part.T, axis=0, keepdims=True)


def odd_self(info_ref, unit_ref, best_ref):
    @pl.when(info_ref[0] == 1)
    def _():
        best_ref[...] = highest(self_part(info_ref[2 + PAIRS], rows_of(unit_ref)))

    @pl.when(info_ref[0] == 0)
    def _():
        best_ref[...] = jnp.full(best_ref.shape, -1.0, jnp.float32)


def pair_scores(info_ref, unit_ref, got_ref, send_ref, over_ref=None):
    odd, mine = info_ref[0], info_ref[1]
    unit = rows_of(unit_ref)
    send_ref[...] = jnp.full(send_ref.shape, -1.0, jnp.float32)
    part = jnp.full((ROWS, 128), -1.0, jnp.float32)
    for p in range(SLOTS):
        code = info_ref[3 + p]
        twice = code == mine
        scores = products(unit, rows_of(got_ref.at[:, p]))
        part = jnp.where(twice, part, folded(part, scores))
        cols = jnp.where(twice, -1.0, jnp.max(scores, axis=0, keepdims=True))
        line = to_reach(code) + jnp.where(odd == 1, 0, GROUP)

        @pl.when(line < 2 * GROUP)
        def _():
            send_ref[line] = jnp.maximum(send_ref[line], cols)

        if over_ref is not None:

            @pl.when(line >= 2 * GROUP)
            def _():
                over_ref[line - 2 * GROUP] = jnp.maximum(over_ref[line - 2 * GROUP], cols)

    return part


def even_scores(info_ref, unit_ref, got_ref, best_ref, send_ref, over_ref):
    over_ref[...] = jnp.full(over_ref.shape, -1.0, jnp.float32)

    @pl.when(info_ref[0] == 0)
    def _():
        part = pair_scores(info_ref, unit_ref, got_ref, send_ref, over_ref)
        best_ref[...] = highest(jnp.maximum(part, self_part(info_ref[2 + PAIRS], rows_of(unit_ref))))


def odd_scores(info_ref, unit_ref, got_ref, self_ref, held_best_ref, held_send_ref, best_ref, send_ref):
    @pl.when(info_ref[0] == 1)
    def _():
        part = pair_scores(info_ref, unit_ref, got_ref, send_ref)
        best_ref[...] = jnp.maximum(highest(part), self_ref[...])

    @pl.when(info_ref[0] == 0)
    def _():
        best_ref[...] = held_best_ref[...]
        send_ref[...] = held_send_ref[...]


def exchange(parts):
    return lax.all_to_all(parts, "shard", 0, 0, axis_index_groups=[ORDER], tiled=True)


def shards(documents, partners, counts):
    n_cluster = lax.axis_size("cluster")
    my_cluster, my_shard = lax.axis_index("cluster"), lax.axis_index("shard")
    odd = my_cluster % 2
    unit = pl.pallas_call(
        normalise,
        in_specs=[ANY] * 3,
        out_specs=ANY,
        out_shape=jax.ShapeDtypeStruct((GROUP, TALL, LANES), jnp.bfloat16),
        scratch_shapes=[
            pltpu.VMEM((ROWS, D), jnp.bfloat16),
            pltpu.VMEM((GROUP, TALL, LANES), jnp.bfloat16),
            pltpu.SMEM((1, PAIRS), jnp.int32),
            pltpu.SMEM((1,), jnp.int32),
            pltpu.SemaphoreType.DMA((ROWS // STEP,)),
            pltpu.SemaphoreType.DMA((ROWS // STEP,)),
            pltpu.SemaphoreType.DMA((2,)),
        ],
    )(partners, counts, documents)
    own = exchange(unit)
    near = lax.ppermute(own, "cluster", [(c, c ^ 1) for c in range(n_cluster)])
    far = lax.ppermute(near, "cluster", [((c + 2) % n_cluster, c) for c in range(1, n_cluster, 2)])
    info = jnp.concatenate([odd[None], my_shard[None], partners[0], counts])
    held, near = lax.optimization_barrier((unit, near))
    self_best = pl.pallas_call(
        odd_self,
        in_specs=[SMEM, VMEM],
        out_specs=VMEM,
        out_shape=jax.ShapeDtypeStruct((1, ROWS), jnp.float32),
        cost_estimate=pl.CostEstimate(flops=2 * ROWS * ROWS * D, bytes_accessed=ROWS * D * 2, transcendentals=0),
        compiler_params=pltpu.CompilerParams(vmem_limit_bytes=12 * 2**20),
    )(info, held)
    table = own[:, BODY, :PAIRS].astype(jnp.int32).reshape(-1)
    picked = pl.pallas_call(
        pick,
        in_specs=[SMEM, SMEM, VMEM, VMEM, VMEM],
        out_specs=VMEM,
        out_shape=jax.ShapeDtypeStruct((GROUP, SLOTS, BODY, LANES), jnp.bfloat16),
        compiler_params=pltpu.CompilerParams(vmem_limit_bytes=16 * 2**20),
    )(table, odd[None], own, near, far)
    picked, info, self_best, is_odd = lax.optimization_barrier((picked, info, self_best, odd == 1))
    got = exchange(picked)
    best_shape = jax.ShapeDtypeStruct((1, ROWS), jnp.float32)
    send_shape = jax.ShapeDtypeStruct((2 * GROUP, 1, ROWS), jnp.float32)
    over_shape = jax.ShapeDtypeStruct((GROUP, 1, ROWS), jnp.float32)
    params = pltpu.CompilerParams(vmem_limit_bytes=12 * 2**20)
    best, send, over = pl.pallas_call(
        even_scores,
        in_specs=[SMEM, VMEM, VMEM],
        out_specs=[VMEM] * 3,
        out_shape=[best_shape, send_shape, over_shape],
        compiler_params=params,
    )(info, unit, got)
    over = lax.ppermute(over, "cluster", [(c, c + 1) for c in range(0, n_cluster, 2)])
    best, send = pl.pallas_call(
        odd_scores,
        in_specs=[SMEM] + [VMEM] * 5,
        out_specs=[VMEM] * 2,
        out_shape=[best_shape, send_shape],
        input_output_aliases={4: 0, 5: 1},
        compiler_params=params,
        cost_estimate=pl.CostEstimate(flops=SLOTS * 2 * ROWS * ROWS * D, bytes_accessed=4 * ROWS * D * 2, transcendentals=0),
    )(info, unit, got, self_best, best, send)
    first = jnp.where(is_odd, jnp.maximum(send[:GROUP], over), send[:GROUP])
    send = jnp.concatenate([first, send[GROUP:]])
    reach = [
        [c * GROUP + s for c in (odd_one, (odd_one + 1) % n_cluster) for s in REACH]
        for odd_one in range(1, n_cluster, 2)
    ]
    back = lax.all_to_all(send, ("cluster", "shard"), 0, 0, axis_index_groups=reach, tiled=True)
    best = jnp.maximum(best[0], jnp.max(back, axis=(0, 1)))
    return jnp.where(jnp.arange(ROWS, dtype=jnp.int32) < counts[0], best, 0.0)


def solution(mesh):
    return jax.shard_map(
        shards,
        mesh=mesh,
        in_specs=(
            P(("cluster", "shard"), None),
            P(("cluster", "shard"), None),
            P(("cluster", "shard")),
        ),
        out_specs=P(("cluster", "shard")),
        check_vma=False,
    )
```

time: 99.3 us -> 95.1 us (0.958)
  blocking collectives: 55.6 us -> 66.9 us
  starting transfers between devices: 23.5 us -> 13.9 us
  waiting for transfers between devices: 6.95 us -> 3.01 us
  other arithmetic: 2.16 us -> 0.86 us
    all_to_all x2 -> x3, blocking collectives: 55.6 us -> 66.9 us  [the longest x2 52.9 us: exchange(): lax.all_to_all(parts, 'shard', 0, 0, axis_index_groups=[ORDER], tiled=True)]
    all_to_all x1 -> x0, starting transfers between devices: 7.76 us -> none  [shards(): lax.all_to_all(send, ('cluster', 'shard'), 0, 0, axis_index_groups=reach,...]
    all_to_all x1 -> x0, waiting for transfers between devices: 3.85 us -> none  [shards(): lax.all_to_all(send, ('cluster', 'shard'), 0, 0, axis_index_groups=reach,...]
    ppermute x1, starting transfers between devices: 15 us -> 12.2 us  [shards(): lax.ppermute(over, 'cluster', [(c, c + 1) for c in range(0, n_cluster, 2)])]
    pallas_call x2, Pallas kernels: 3.24 us -> 1.13 us  [the longest x1 0.57 us: shards(): pl.pallas_call(odd_scores, in_specs=[SMEM] + [VMEM] * 5, out_specs=[VMEM]...]
  transfers between devices with their start and end apart: 4 -> 3, of which waited for: 3 -> 2; matrix products, arithmetic and copies ran while one was open for 1% -> 0% of each run, Pallas kernels for 3% -> 1%
where the time goes in v5:
time: 95.1 us; the launch traced here: 94.7 us
  blocking collectives  66.9 us (70%)
  starting transfers between devices  13.9 us (15%)
  Pallas kernels  9.16 us (10%)
  waiting for transfers between devices  3.01 us (3%)
    all_to_all x2, blocking collectives, exchange(): lax.all_to_all(parts, 'shard', 0, 0, axis_index_groups=[ORDER], tiled=True)  52.9 us
    all_to_all x1, blocking collectives, shards(): lax.all_to_all(send, ('cluster', 'shard'), 0, 0, axis_index_groups=reach,...  14 us
    ppermute x1, starting transfers between devices, shards(): lax.ppermute(over, 'cluster', [(c, c + 1) for c in range(0, n_cluster, 2)])  12.2 us
    pallas_call x1, Pallas kernels, shards(): pl.pallas_call(even_scores, in_specs=[SMEM, VMEM, VMEM], out_specs=[VMEM]...  3.63 us
    ppermute x1, waiting for transfers between devices, shards(): near = lax.ppermute(own, 'cluster', [(c, c ^ 1) for c in range(n_cluster)])  2.75 us
    pallas_call x1, Pallas kernels, shards(): pl.pallas_call(normalise, in_specs=[ANY] * 3, out_specs=ANY, out_shape=ja...  2.36 us
    pallas_call x1, Pallas kernels, shards(): pl.pallas_call(pick, in_specs=[SMEM, SMEM, VMEM, VMEM, VMEM], out_specs=V...  2.04 us
  transfers between devices with their start and end apart: 3, of which 2 were waited for; matrix products, arithmetic and copies ran while one was open for 0% of the time, Pallas kernels for 1%

profile of v5, /device:TPU:0, one launch (start us, length us, event | category | flops | bytes accessed | tf_op | source)
XLA Modules:
  0.0 94.7 jit_solution(6329168654848844227)
XLA Ops:
  0.7 2.4 %shard_map.37.unit_ref = bf16[16,272,128]{2,1,0:T(8,128)(2,1)} custom-call(s32[1,4]{1,0:T(1,128)} %partners_ref.1, s32[1]{0:T(128)} %copy.8.counts_ref, bf16[512,1024]{1,0:T(8,128)(2,1)} %doc_ref.1), custom_call_target="tpu_custom_call" | custom-call | tf_op jit(solution)/shard_map/pallas_call | solution.py:202
  3.0 0.0 copy-start.1
  3.0 0.0 copy-start
  3.0 23.1 %all_to_all.15.own_ref = bf16[16,272,128]{2,1,0:T(8,128)(2,1)S(1)} all-to-all(bf16[16,272,128]{2,1,0:T(8,128)(2,1)} %shard_map.37.unit_ref), channel_id=1, replica_groups={{10,15,13,11,2,14,6,7,0,9,5,4,8,1,3,12},{26,31,29,27,18,30,22,23,16,25,..., dimensions={0} | all-to-all | bytes 2228224 | tf_op jit(solution)/shard_map/all_to_all | solution.py:195
  26.1 0.0 collective-permute-start
  26.1 2.8 %collective-permute-done.near_ref = bf16[16,272,128]{2,1,0:T(8,128)(2,1)S(1)} collective-permute-done((bf16[16,272,128]{2,1,0:T(8,128)(2,1)S(1)}, bf16[16,272,128]{2,1,0:T(8,128)(2,1)S(1)}, u32[]{:S(2)}, u32[]{:S(2)}) %collective-permute-start) | collective-permute-done | bytes 1114144 | tf_op jit(solution)/shard_map/ppermute | solution.py:218
  28.9 1.7 %collective-permute-start.1 = (bf16[16,272,128]{2,1,0:T(8,128)(2,1)S(1)}, bf16[16,272,128]{2,1,0:T(8,128)(2,1)}, u32[]{:S(2)}, u32[]{:S(2)}) collective-permute-start(bf16[16,272,128]{2,1,0:T(8,128)(2,1)S(1)} %collective-permute-done.near_ref), channel_id=1, source_target_pairs={{48,16},{80,48},{112,80},{16,112},{49,17},{81,49},{113,81},{17,113... | collective-permute-start | bytes 3342344 | tf_op jit(solution)/shard_map/ppermute | solution.py:219
  30.6 0.0 copy-done.1
  30.6 0.1 pad_add_fusion.info_ref
  30.7 0.1 reshape.4.table_ref
  30.8 0.0 copy-done
  30.8 0.6 shard_map.39.self_ref
  31.4 0.0 collective-permute-done.1.far_ref
  31.4 2.0 %shard_map.38 = bf16[16,3,256,128]{3,2,1,0:T(8,128)(2,1)S(1)} custom-call(s32[64]{0:T(128)S(1)} %reshape.4.table_ref, s32[1]{0:T(128)} %bitcast.1.odd_ref, bf16[16,272,128]{2,1,0:T(8,128)(2,1)S(1)} %all_to_all.15.own_ref, bf16[16,272,128]{2,1,0:T(8,128)(2,1)S(1)} %collective-permute-done.near_ref, bf16[16,272,128]{2,1,0:T(8,128)(2,1)} %collective-permute-done.1.far_ref), custom_call_target="tpu_custom_call" | custom-call | tf_op jit(solution)/shard_map/pallas_call | solution.py:231
  33.4 29.8 %all_to_all.16.got_ref = bf16[16,3,256,128]{3,2,1,0:T(8,128)(2,1)S(1)} all-to-all(bf16[16,3,256,128]{3,2,1,0:T(8,128)(2,1)S(1)} %shard_map.38), channel_id=1, replica_groups={{10,15,13,11,2,14,6,7,0,9,5,4,8,1,3,12},{26,31,29,27,18,30,22,23,16,25,..., dimensions={0} | all-to-all | bytes 6291456 | tf_op jit(solution)/shard_map/all_to_all | solution.py:195
  63.2 3.6 %shard_map.40 = (f32[1,512]{1,0:T(1,128)S(1)}, f32[32,1,512]{2,1,0:T(1,128)S(1)}, f32[16,1,512]{2,1,0:T(1,128)S(1)}) custom-call(s32[7]{0:T(128)S(1)} %pad_add_fusion.info_ref, bf16[16,272,128]{2,1,0:T(8,128)(2,1)S(1)} %copy-done, bf16[16,3,256,128]{3,2,1,0:T(8,128)(2,1)S(1)} %all_to_all.16.got_ref), custom_call_target="tpu_custom_call" | custom-call | tf_op jit(solution)/shard_map/pallas_call | solution.py:244
  66.9 12.2 %collective-permute-start.2 = (f32[16,1,512]{2,1,0:T(1,128)S(1)}, f32[16,1,512]{2,1,0:T(1,128)S(1)}, u32[]{:S(2)}, u32[]{:S(2)}) collective-permute-start(f32[16,1,512]{2,1,0:T(1,128)S(1)} %get-tuple-element.26), channel_id=1, source_target_pairs={{0,16},{32,48},{64,80},{96,112},{1,17},{33,49},{65,81},{97,113},{2... | collective-permute-start | bytes 98312 | tf_op jit(solution)/shard_map/ppermute | solution.py:251
  79.1 0.6 shard_map.41
  79.7 0.3 collective-permute-done.2
  80.0 0.1 pad_maximum_fusion
  80.0 14.0 %all_to_all.17 = f32[32,1,512]{2,1,0:T(1,128)S(1)} all-to-all(f32[32,1,512]{2,1,0:T(1,128)S(1)} %pad_maximum_fusion), channel_id=1, replica_groups={{26,31,29,27,18,30,22,23,16,25,21,20,24,17,19,28,42,47,45,43,34,46,38,3..., dimensions={0} | all-to-all | bytes 131072 | tf_op jit(solution)/shard_map/all_to_all | solution.py:267
  94.1 0.1 reduce_max.9
  94.1 0.6 maximum_select_fusion
  (2 shorter events, 0.1 us)
Async XLA Ops:
  3.0 27.6 %copy-start.1 = (s32[1,4]{1,0:T(1,128)S(1)}, s32[1,4]{1,0:T(1,128)}, u32[]{:S(2)}) copy-start(s32[1,4]{1,0:T(1,128)} %partners_ref.1) | copy-start | bytes 52
  3.0 27.8 %copy-start = (bf16[16,272,128]{2,1,0:T(8,128)(2,1)S(1)}, bf16[16,272,128]{2,1,0:T(8,128)(2,1)}, u32[]{:S(2)}) copy-start(bf16[16,272,128]{2,1,0:T(8,128)(2,1)} %shard_map.37.unit_ref) | copy-start | bytes 3342340
  26.1 2.8 %collective-permute-start = (bf16[16,272,128]{2,1,0:T(8,128)(2,1)S(1)}, bf16[16,272,128]{2,1,0:T(8,128)(2,1)S(1)}, u32[]{:S(2)}, u32[]{:S(2)}) collective-permute-start(bf16[16,272,128]{2,1,0:T(8,128)(2,1)S(1)} %all_to_all.15.own_ref), channel_id=1, source_target_pairs={{0,16},{16,0},{32,48},{48,32},{64,80},{80,64},{96,112},{112,96},{1... | collective-permute-start | bytes 3342344 | tf_op jit(solution)/shard_map/ppermute | solution.py:218
  28.9 2.5 %collective-permute-start.1 = (bf16[16,272,128]{2,1,0:T(8,128)(2,1)S(1)}, bf16[16,272,128]{2,1,0:T(8,128)(2,1)}, u32[]{:S(2)}, u32[]{:S(2)}) collective-permute-start(bf16[16,272,128]{2,1,0:T(8,128)(2,1)S(1)} %collective-permute-done.near_ref), channel_id=1, source_target_pairs={{48,16},{80,48},{112,80},{16,112},{49,17},{81,49},{113,81},{17,113... | collective-permute-start | bytes 3342344 | tf_op jit(solution)/shard_map/ppermute | solution.py:219
  66.9 13.0 %collective-permute-start.2 = (f32[16,1,512]{2,1,0:T(1,128)S(1)}, f32[16,1,512]{2,1,0:T(1,128)S(1)}, u32[]{:S(2)}, u32[]{:S(2)}) collective-permute-start(f32[16,1,512]{2,1,0:T(1,128)S(1)} %get-tuple-element.26), channel_id=1, source_target_pairs={{0,16},{32,48},{64,80},{96,112},{1,17},{33,49},{65,81},{97,113},{2... | collective-permute-start | bytes 98312 | tf_op jit(solution)/shard_map/ppermute | solution.py:251

commit v6 on v5

--- a/solution.py
+++ b/solution.py
@@ -15,7 +15,7 @@
 TILES = D // LANES
 BODY = TILES * CUT
 TALL = BODY + 16
-STEP = 128
+STEP = 256
 ORDER = [10, 15, 13, 11, 2, 14, 6, 7, 0, 9, 5, 4, 8, 1, 3, 12]
 REACH = ORDER
 PLACE = [ORDER.index(s) for s in range(GROUP)]
@@ -46,7 +46,7 @@
     return raw * lax.rsqrt(jnp.sum(raw * raw, axis=1, keepdims=True) + 1e-06)
 
 
-def normalise(partners_ref, counts_ref, doc_ref, out_ref, raw, unit, partners, counts, in_sem, out_sem, small_sem):
+def normalise(partners_ref, counts_ref, doc_ref, unit, raw, partners, counts, in_sem, small_sem):
     small = [
         pltpu.make_async_copy(partners_ref, partners, small_sem.at[0]),
         pltpu.make_async_copy(counts_ref, counts, small_sem.at[1]),
@@ -54,10 +54,6 @@
     fetch = [
         pltpu.make_async_copy(doc_ref.at[pl.ds(i, STEP)], raw.at[pl.ds(i, STEP)], in_sem.at[i // STEP])
         for i in range(0, ROWS, STEP)
-    ]
-    store = [
-        pltpu.make_async_copy(unit.at[pl.ds(i, STEP // CUT)], out_ref.at[pl.ds(i, STEP // CUT)], out_sem.at[i * CUT // STEP])
-        for i in range(0, GROUP, STEP // CUT)
     ]
     for copy in small + fetch:
         copy.start()
@@ -80,32 +76,43 @@
             for t in range(TILES):
                 unit[at, t * CUT : (t + 1) * CUT] = rows[j : j + CUT, t * LANES : (t + 1) * LANES]
             unit[at, BODY:] = entry
-        store[i // STEP].start()
-    for copy in store:
-        copy.wait()
-
-
-def pick(table_ref, odd_ref, own_ref, near_ref, far_ref, out_ref):
-    def all_from(next_ref):
+
+
+def pick(table_ref, odd_ref, own_ref, near_ref, far_ref, out_ref, far, sem):
+    fetch = pltpu.make_async_copy(far_ref, far, sem)
+
+    def each(body):
         for e in range(GROUP * SLOTS):
             dst, slot = e // SLOTS, e % SLOTS
-            code = table_ref[dst * PAIRS + 1 + slot]
-
-            @pl.when(code < GROUP)
-            def _():
-                out_ref[dst, slot] = own_ref[code, :BODY]
-
+            body(dst, slot, table_ref[dst * PAIRS + 1 + slot])
+
+    def from_own(dst, slot, code):
+        @pl.when(code < GROUP)
+        def _():
+            out_ref[dst, slot] = own_ref[code, :BODY]
+
+    def from_next(next_ref):
+        def one(dst, slot, code):
             @pl.when(code >= GROUP)
             def _():
                 out_ref[dst, slot] = next_ref[code - GROUP, :BODY]
 
+        return one
+
+    @pl.when(odd_ref[0] == 1)
+    def _():
+        fetch.start()
+
+    each(from_own)
+
     @pl.when(odd_ref[0] == 0)
     def _():
-        all_from(near_ref)
+        each(from_next(near_ref))
 
     @pl.when(odd_ref[0] == 1)
     def _():
-        all_from(far_ref)
+        fetch.wait()
+        each(from_next(far))
 
 
 def rows_of(slices):
@@ -202,23 +209,21 @@
     unit = pl.pallas_call(
         normalise,
         in_specs=[ANY] * 3,
-        out_specs=ANY,
+        out_specs=VMEM,
         out_shape=jax.ShapeDtypeStruct((GROUP, TALL, LANES), jnp.bfloat16),
         scratch_shapes=[
             pltpu.VMEM((ROWS, D), jnp.bfloat16),
-            pltpu.VMEM((GROUP, TALL, LANES), jnp.bfloat16),
             pltpu.SMEM((1, PAIRS), jnp.int32),
             pltpu.SMEM((1,), jnp.int32),
             pltpu.SemaphoreType.DMA((ROWS // STEP,)),
-            pltpu.SemaphoreType.DMA((ROWS // STEP,)),
             pltpu.SemaphoreType.DMA((2,)),
         ],
+        compiler_params=pltpu.CompilerParams(vmem_limit_bytes=8 * 2**20),
     )(partners, counts, documents)
     own = exchange(unit)
     near = lax.ppermute(own, "cluster", [(c, c ^ 1) for c in range(n_cluster)])
-    far = lax.ppermute(near, "cluster", [((c + 2) % n_cluster, c) for c in range(1, n_cluster, 2)])
     info = jnp.concatenate([odd[None], my_shard[None], partners[0], counts])
-    held, near = lax.optimization_barrier((unit, near))
+    held, own = lax.optimization_barrier((unit, own))
     self_best = pl.pallas_call(
         odd_self,
         in_specs=[SMEM, VMEM],
@@ -227,11 +232,14 @@
         cost_estimate=pl.CostEstimate(flops=2 * ROWS * ROWS * D, bytes_accessed=ROWS * D * 2, transcendentals=0),
         compiler_params=pltpu.CompilerParams(vmem_limit_bytes=12 * 2**20),
     )(info, held)
+    near, self_best = lax.optimization_barrier((near, self_best))
+    far = lax.ppermute(near, "cluster", [((c + 2) % n_cluster, c) for c in range(1, n_cluster, 2)])
     table = own[:, BODY, :PAIRS].astype(jnp.int32).reshape(-1)
     picked = pl.pallas_call(
         pick,
-        in_specs=[SMEM, SMEM, VMEM, VMEM, VMEM],
+        in_specs=[SMEM, SMEM, VMEM, VMEM, ANY],
         out_specs=VMEM,
+        scratch_shapes=[pltpu.VMEM((GROUP, TALL, LANES), jnp.bfloat16), pltpu.SemaphoreType.DMA],
         out_shape=jax.ShapeDtypeStruct((GROUP, SLOTS, BODY, LANES), jnp.bfloat16),
         compiler_params=pltpu.CompilerParams(vmem_limit_bytes=16 * 2**20),
     )(table, odd[None], own, near, far)
@@ -248,7 +256,7 @@
         out_shape=[best_shape, send_shape, over_shape],
         compiler_params=params,
     )(info, unit, got)
-    over = lax.ppermute(over, "cluster", [(c, c + 1) for c in range(0, n_cluster, 2)])
+    over = lax.ppermute(over, "cluster", [(c, c ^ 1) for c in range(n_cluster)])
     best, send = pl.pallas_call(
         odd_scores,
         in_specs=[SMEM] + [VMEM] * 5,

time: 95.1 us -> 92.5 us (0.973)
  local copies, waits for them, and re-layouts: 0.09 us -> 1.96 us
  Pallas kernels: 9.16 us -> 7.31 us
  blocking collectives: 66.9 us -> 65.1 us
    all_to_all x2, blocking collectives: 52.9 us -> 50.5 us  [exchange(): lax.all_to_all(parts, 'shard', 0, 0, axis_index_groups=[ORDER], tiled=True)]
    unnamed x4 -> x6, local copies, waits for them, and re-layouts: 0.01 us -> 1.88 us
    pallas_call x2, Pallas kernels: 4.4 us -> 2.55 us  [the longest x1 1.49 us: shards(): pl.pallas_call(pick, in_specs=[SMEM, SMEM, VMEM, VMEM, ANY], out_specs=VM...]
where the time goes in v6:
time: 92.5 us; the launch traced here: 92.2 us
  blocking collectives  65.1 us (70%)
  starting transfers between devices  13.8 us (15%)
  Pallas kernels  7.31 us (8%)
  waiting for transfers between devices  2.39 us (3%)
  local copies, waits for them, and re-layouts  1.96 us (2%)
    all_to_all x2, blocking collectives, exchange(): lax.all_to_all(parts, 'shard', 0, 0, axis_index_groups=[ORDER], tiled=True)  50.5 us
    all_to_all x1, blocking collectives, shards(): lax.all_to_all(send, ('cluster', 'shard'), 0, 0, axis_index_groups=reach,...  14.6 us
    ppermute x1, starting transfers between devices, shards(): over = lax.ppermute(over, 'cluster', [(c, c ^ 1) for c in range(n_cluster)])  12.2 us
    pallas_call x1, Pallas kernels, shards(): pl.pallas_call(even_scores, in_specs=[SMEM, VMEM, VMEM], out_specs=[VMEM]...  3.64 us
    ppermute x1, waiting for transfers between devices, shards(): near = lax.ppermute(own, 'cluster', [(c, c ^ 1) for c in range(n_cluster)])  2.11 us
    unnamed x6, local copies, waits for them, and re-layouts  1.88 us
  transfers between devices with their start and end apart: 3, of which 2 were waited for; matrix products, arithmetic and copies ran while one was open for 0% of the time, Pallas kernels for 1%

profile of v6, /device:TPU:0, one launch (start us, length us, event | category | flops | bytes accessed | tf_op | source)
XLA Modules:
  0.0 92.2 jit_solution(17205234891597324368)
XLA Ops:
  0.7 0.0 copy-start
  0.7 1.2 %copy-done = bf16[512,1024]{1,0:T(8,128)(2,1)S(1)} copy-done((bf16[512,1024]{1,0:T(8,128)(2,1)S(1)}, bf16[512,1024]{1,0:T(8,128)(2,1)}, u32[]{:S(2)}) %copy-start) | copy-done | bytes 1048600
  1.9 0.7 copy-done.1
  2.5 1.1 %shard_map.37.unit_ref = bf16[16,272,128]{2,1,0:T(8,128)(2,1)S(1)} custom-call(s32[1,4]{1,0:T(1,128)S(1)} %copy-done.1, s32[1]{0:T(128)} %copy.8.counts_ref, bf16[512,1024]{1,0:T(8,128)(2,1)S(1)} %copy-done), custom_call_target="tpu_custom_call" | custom-call | tf_op jit(solution)/shard_map/pallas_call | solution.py:209
  3.6 0.0 copy-start.2
  3.6 22.5 %all_to_all.15.own_ref = bf16[16,272,128]{2,1,0:T(8,128)(2,1)S(1)} all-to-all(bf16[16,272,128]{2,1,0:T(8,128)(2,1)S(1)} %shard_map.37.unit_ref), channel_id=1, replica_groups={{10,15,13,11,2,14,6,7,0,9,5,4,8,1,3,12},{26,31,29,27,18,30,22,23,16,25,..., dimensions={0} | all-to-all | bytes 2228224 | tf_op jit(solution)/shard_map/all_to_all | solution.py:202
  26.2 0.0 collective-permute-start
  26.2 0.0 copy-done.2
  26.2 0.1 pad_add_fusion.info_ref
  26.2 0.6 shard_map.38.self_ref
  26.8 2.1 %collective-permute-done.near_ref = bf16[16,272,128]{2,1,0:T(8,128)(2,1)S(1)} collective-permute-done((bf16[16,272,128]{2,1,0:T(8,128)(2,1)S(1)}, bf16[16,272,128]{2,1,0:T(8,128)(2,1)S(1)}, u32[]{:S(2)}, u32[]{:S(2)}) %collective-permute-start) | collective-permute-done | bytes 1114144 | tf_op jit(solution)/shard_map/ppermute | solution.py:224
  28.9 1.6 %collective-permute-start.1 = (bf16[16,272,128]{2,1,0:T(8,128)(2,1)S(1)}, bf16[16,272,128]{2,1,0:T(8,128)(2,1)}, u32[]{:S(2)}, u32[]{:S(2)}) collective-permute-start(bf16[16,272,128]{2,1,0:T(8,128)(2,1)S(1)} %collective-permute-done.near_ref), channel_id=1, source_target_pairs={{48,16},{80,48},{112,80},{16,112},{49,17},{81,49},{113,81},{17,113... | collective-permute-start | bytes 3342344 | tf_op jit(solution)/shard_map/ppermute | solution.py:236
  30.6 0.1 reshape.4.table_ref
  30.7 0.0 collective-permute-done.1.far_ref
  30.7 1.5 %shard_map.39 = bf16[16,3,256,128]{3,2,1,0:T(8,128)(2,1)S(1)} custom-call(s32[64]{0:T(128)S(1)} %reshape.4.table_ref, s32[1]{0:T(128)} %bitcast.1.odd_ref, bf16[16,272,128]{2,1,0:T(8,128)(2,1)S(1)} %all_to_all.15.own_ref, bf16[16,272,128]{2,1,0:T(8,128)(2,1)S(1)} %collective-permute-done.near_ref, bf16[16,272,128]{2,1,0:T(8,128)(2,1)} %collective-permute-done.1.far_ref), custom_call_target="tpu_custom_call" | custom-call | tf_op jit(solution)/shard_map/pallas_call | solution.py:238
  32.2 28.0 %all_to_all.16.got_ref = bf16[16,3,256,128]{3,2,1,0:T(8,128)(2,1)S(1)} all-to-all(bf16[16,3,256,128]{3,2,1,0:T(8,128)(2,1)S(1)} %shard_map.39), channel_id=1, replica_groups={{10,15,13,11,2,14,6,7,0,9,5,4,8,1,3,12},{26,31,29,27,18,30,22,23,16,25,..., dimensions={0} | all-to-all | bytes 6291456 | tf_op jit(solution)/shard_map/all_to_all | solution.py:202
  60.1 3.6 %shard_map.40 = (f32[1,512]{1,0:T(1,128)S(1)}, f32[32,1,512]{2,1,0:T(1,128)S(1)}, f32[16,1,512]{2,1,0:T(1,128)S(1)}) custom-call(s32[7]{0:T(128)S(1)} %pad_add_fusion.info_ref, bf16[16,272,128]{2,1,0:T(8,128)(2,1)S(1)} %shard_map.37.unit_ref, bf16[16,3,256,128]{3,2,1,0:T(8,128)(2,1)S(1)} %all_to_all.16.got_ref), custom_call_target="tpu_custom_call" | custom-call | tf_op jit(solution)/shard_map/pallas_call | solution.py:252
  63.8 12.2 %collective-permute-start.2 = (f32[16,1,512]{2,1,0:T(1,128)S(1)}, f32[16,1,512]{2,1,0:T(1,128)S(1)}, u32[]{:S(2)}, u32[]{:S(2)}) collective-permute-start(f32[16,1,512]{2,1,0:T(1,128)S(1)} %get-tuple-element.30), channel_id=1, source_target_pairs={{0,16},{16,0},{32,48},{48,32},{64,80},{80,64},{96,112},{112,96},{1... | collective-permute-start | bytes 98312 | tf_op jit(solution)/shard_map/ppermute | solution.py:259
  76.0 0.6 shard_map.41
  76.5 0.3 collective-permute-done.2
  76.9 0.1 pad_maximum_fusion
  76.9 14.6 %all_to_all.17 = f32[32,1,512]{2,1,0:T(1,128)S(1)} all-to-all(f32[32,1,512]{2,1,0:T(1,128)S(1)} %pad_maximum_fusion), channel_id=1, replica_groups={{26,31,29,27,18,30,22,23,16,25,21,20,24,17,19,28,42,47,45,43,34,46,38,3..., dimensions={0} | all-to-all | bytes 131072 | tf_op jit(solution)/shard_map/all_to_all | solution.py:275
  91.6 0.1 reduce_max.9
  91.6 0.6 maximum_select_fusion
  (3 shorter events, 0.1 us)
Async XLA Ops:
  0.7 1.2 %copy-start = (bf16[512,1024]{1,0:T(8,128)(2,1)S(1)}, bf16[512,1024]{1,0:T(8,128)(2,1)}, u32[]{:S(2)}) copy-start(bf16[512,1024]{1,0:T(8,128)(2,1)} %doc_ref.1) | copy-start | bytes 3145732
  1.9 0.7 copy-start.1
  3.6 22.6 %copy-start.2 = (s32[1,4]{1,0:T(1,128)S(1)}, s32[1,4]{1,0:T(1,128)}, u32[]{:S(2)}) copy-start(s32[1,4]{1,0:T(1,128)} %partners_ref.1) | copy-start | bytes 52
  26.2 2.8 %collective-permute-start = (bf16[16,272,128]{2,1,0:T(8,128)(2,1)S(1)}, bf16[16,272,128]{2,1,0:T(8,128)(2,1)S(1)}, u32[]{:S(2)}, u32[]{:S(2)}) collective-permute-start(bf16[16,272,128]{2,1,0:T(8,128)(2,1)S(1)} %all_to_all.15.own_ref), channel_id=1, source_target_pairs={{0,16},{16,0},{32,48},{48,32},{64,80},{80,64},{96,112},{112,96},{1... | collective-permute-start | bytes 3342344 | tf_op jit(solution)/shard_map/ppermute | solution.py:224
  28.9 1.8 %collective-permute-start.1 = (bf16[16,272,128]{2,1,0:T(8,128)(2,1)S(1)}, bf16[16,272,128]{2,1,0:T(8,128)(2,1)}, u32[]{:S(2)}, u32[]{:S(2)}) collective-permute-start(bf16[16,272,128]{2,1,0:T(8,128)(2,1)S(1)} %collective-permute-done.near_ref), channel_id=1, source_target_pairs={{48,16},{80,48},{112,80},{16,112},{49,17},{81,49},{113,81},{17,113... | collective-permute-start | bytes 3342344 | tf_op jit(solution)/shard_map/ppermute | solution.py:236
  63.8 13.0 %collective-permute-start.2 = (f32[16,1,512]{2,1,0:T(1,128)S(1)}, f32[16,1,512]{2,1,0:T(1,128)S(1)}, u32[]{:S(2)}, u32[]{:S(2)}) collective-permute-start(f32[16,1,512]{2,1,0:T(1,128)S(1)} %get-tuple-element.30), channel_id=1, source_target_pairs={{0,16},{16,0},{32,48},{48,32},{64,80},{80,64},{96,112},{112,96},{1... | collective-permute-start | bytes 98312 | tf_op jit(solution)/shard_map/ppermute | solution.py:259

commit v7 on v6

--- a/solution.py
+++ b/solution.py
@@ -78,9 +78,7 @@
             unit[at, BODY:] = entry
 
 
-def pick(table_ref, odd_ref, own_ref, near_ref, far_ref, out_ref, far, sem):
-    fetch = pltpu.make_async_copy(far_ref, far, sem)
-
+def pick(table_ref, info_ref, own_ref, near_ref, far_ref, out_ref):
     def each(body):
         for e in range(GROUP * SLOTS):
             dst, slot = e // SLOTS, e % SLOTS
@@ -99,20 +97,15 @@
 
         return one
 
-    @pl.when(odd_ref[0] == 1)
-    def _():
-        fetch.start()
-
     each(from_own)
 
-    @pl.when(odd_ref[0] == 0)
+    @pl.when(info_ref[0] == 0)
     def _():
         each(from_next(near_ref))
 
-    @pl.when(odd_ref[0] == 1)
-    def _():
-        fetch.wait()
-        each(from_next(far))
+    @pl.when(info_ref[0] == 1)
+    def _():
+        each(from_next(far_ref))
 
 
 def rows_of(slices):
@@ -232,18 +225,17 @@
         cost_estimate=pl.CostEstimate(flops=2 * ROWS * ROWS * D, bytes_accessed=ROWS * D * 2, transcendentals=0),
         compiler_params=pltpu.CompilerParams(vmem_limit_bytes=12 * 2**20),
     )(info, held)
-    near, self_best = lax.optimization_barrier((near, self_best))
+    table = own[:, BODY, :PAIRS].astype(jnp.int32).reshape(-1)
+    near, self_best, table, info, is_odd = lax.optimization_barrier((near, self_best, table, info, odd == 1))
     far = lax.ppermute(near, "cluster", [((c + 2) % n_cluster, c) for c in range(1, n_cluster, 2)])
-    table = own[:, BODY, :PAIRS].astype(jnp.int32).reshape(-1)
     picked = pl.pallas_call(
         pick,
-        in_specs=[SMEM, SMEM, VMEM, VMEM, ANY],
+        in_specs=[SMEM, SMEM, VMEM, VMEM, VMEM],
         out_specs=VMEM,
-        scratch_shapes=[pltpu.VMEM((GROUP, TALL, LANES), jnp.bfloat16), pltpu.SemaphoreType.DMA],
         out_shape=jax.ShapeDtypeStruct((GROUP, SLOTS, BODY, LANES), jnp.bfloat16),
-        compiler_params=pltpu.CompilerParams(vmem_limit_bytes=16 * 2**20),
-    )(table, odd[None], own, near, far)
-    picked, info, self_best, is_odd = lax.optimization_barrier((picked, info, self_best, odd == 1))
+        compiler_params=pltpu.CompilerParams(vmem_limit_bytes=8 * 2**20),
+    )(table, info, own, near, far)
+    picked, info, self_best, is_odd = lax.optimization_barrier((picked, info, self_best, is_odd))
     got = exchange(picked)
     best_shape = jax.ShapeDtypeStruct((1, ROWS), jnp.float32)
     send_shape = jax.ShapeDtypeStruct((2 * GROUP, 1, ROWS), jnp.float32)

time: 92.5 us -> 91.4 us (0.988)
  no operation moved by 1% of the time
where the time goes in v7:
time: 91.4 us; the launch traced here: 91.2 us
  blocking collectives  64.8 us (71%)
  starting transfers between devices  13.2 us (14%)
  Pallas kernels  7.31 us (8%)
  waiting for transfers between devices  2.27 us (2%)
  local copies, waits for them, and re-layouts  1.96 us (2%)
    all_to_all x2, blocking collectives, exchange(): lax.all_to_all(parts, 'shard', 0, 0, axis_index_groups=[ORDER], tiled=True)  50.2 us
    all_to_all x1, blocking collectives, shards(): lax.all_to_all(send, ('cluster', 'shard'), 0, 0, axis_index_groups=reach,...  14.6 us
    ppermute x1, starting transfers between devices, shards(): over = lax.ppermute(over, 'cluster', [(c, c ^ 1) for c in range(n_cluster)])  12.5 us
    pallas_call x1, Pallas kernels, shards(): pl.pallas_call(even_scores, in_specs=[SMEM, VMEM, VMEM], out_specs=[VMEM]...  3.64 us
    ppermute x1, waiting for transfers between devices, shards(): near = lax.ppermute(own, 'cluster', [(c, c ^ 1) for c in range(n_cluster)])  1.98 us
    unnamed x6, local copies, waits for them, and re-layouts  1.88 us
  transfers between devices with their start and end apart: 3, of which 2 were waited for; matrix products, arithmetic and copies ran while one was open for 0% of the time, Pallas kernels for 1%

profile of v7, /device:TPU:0, one launch (start us, length us, event | category | flops | bytes accessed | tf_op | source)
XLA Modules:
  0.0 91.2 jit_solution(13766792063749702518)
XLA Ops:
  0.7 0.0 copy-start
  0.7 1.2 %copy-done = bf16[512,1024]{1,0:T(8,128)(2,1)S(1)} copy-done((bf16[512,1024]{1,0:T(8,128)(2,1)S(1)}, bf16[512,1024]{1,0:T(8,128)(2,1)}, u32[]{:S(2)}) %copy-start) | copy-done | bytes 1048600
  1.9 0.7 copy-done.1
  2.5 1.1 %shard_map.37.unit_ref = bf16[16,272,128]{2,1,0:T(8,128)(2,1)S(1)} custom-call(s32[1,4]{1,0:T(1,128)S(1)} %copy-done.1, s32[1]{0:T(128)} %copy.8.counts_ref, bf16[512,1024]{1,0:T(8,128)(2,1)S(1)} %copy-done), custom_call_target="tpu_custom_call" | custom-call | tf_op jit(solution)/shard_map/pallas_call | solution.py:202
  3.6 0.0 copy-start.2
  3.6 22.5 %all_to_all.15.own_ref = bf16[16,272,128]{2,1,0:T(8,128)(2,1)S(1)} all-to-all(bf16[16,272,128]{2,1,0:T(8,128)(2,1)S(1)} %shard_map.37.unit_ref), channel_id=1, replica_groups={{10,15,13,11,2,14,6,7,0,9,5,4,8,1,3,12},{26,31,29,27,18,30,22,23,16,25,..., dimensions={0} | all-to-all | bytes 2228224 | tf_op jit(solution)/shard_map/all_to_all | solution.py:195
  26.2 0.0 collective-permute-start
  26.2 0.0 copy-done.2
  26.2 0.1 pad_add_fusion.info_ref
  26.3 0.1 reshape.4.table_ref
  26.4 0.6 shard_map.38.self_ref
  26.9 2.0 %collective-permute-done.near_ref = bf16[16,272,128]{2,1,0:T(8,128)(2,1)S(1)} collective-permute-done((bf16[16,272,128]{2,1,0:T(8,128)(2,1)S(1)}, bf16[16,272,128]{2,1,0:T(8,128)(2,1)S(1)}, u32[]{:S(2)}, u32[]{:S(2)}) %collective-permute-start) | collective-permute-done | bytes 1114144 | tf_op jit(solution)/shard_map/ppermute | solution.py:217
  28.9 0.7 collective-permute-start.1
  29.6 0.0 collective-permute-done.1.far_ref
  29.7 1.5 %shard_map.39 = bf16[16,3,256,128]{3,2,1,0:T(8,128)(2,1)S(1)} custom-call(s32[64]{0:T(128)S(1)} %reshape.4.table_ref, s32[7]{0:T(128)S(1)} %pad_add_fusion.info_ref, bf16[16,272,128]{2,1,0:T(8,128)(2,1)S(1)} %all_to_all.15.own_ref, bf16[16,272,128]{2,1,0:T(8,128)(2,1)S(1)} %collective-permute-done.near_ref, ...), custom_call_target="tpu_custom_call" | custom-call | tf_op jit(solution)/shard_map/pallas_call | solution.py:231
  31.1 27.7 %all_to_all.16.got_ref = bf16[16,3,256,128]{3,2,1,0:T(8,128)(2,1)S(1)} all-to-all(bf16[16,3,256,128]{3,2,1,0:T(8,128)(2,1)S(1)} %shard_map.39), channel_id=1, replica_groups={{10,15,13,11,2,14,6,7,0,9,5,4,8,1,3,12},{26,31,29,27,18,30,22,23,16,25,..., dimensions={0} | all-to-all | bytes 6291456 | tf_op jit(solution)/shard_map/all_to_all | solution.py:195
  58.8 3.6 %shard_map.40 = (f32[1,512]{1,0:T(1,128)S(1)}, f32[32,1,512]{2,1,0:T(1,128)S(1)}, f32[16,1,512]{2,1,0:T(1,128)S(1)}) custom-call(s32[7]{0:T(128)S(1)} %pad_add_fusion.info_ref, bf16[16,272,128]{2,1,0:T(8,128)(2,1)S(1)} %shard_map.37.unit_ref, bf16[16,3,256,128]{3,2,1,0:T(8,128)(2,1)S(1)} %all_to_all.16.got_ref), custom_call_target="tpu_custom_call" | custom-call | tf_op jit(solution)/shard_map/pallas_call | solution.py:244
  62.5 12.5 %collective-permute-start.2 = (f32[16,1,512]{2,1,0:T(1,128)S(1)}, f32[16,1,512]{2,1,0:T(1,128)S(1)}, u32[]{:S(2)}, u32[]{:S(2)}) collective-permute-start(f32[16,1,512]{2,1,0:T(1,128)S(1)} %get-tuple-element.36), channel_id=1, source_target_pairs={{0,16},{16,0},{32,48},{48,32},{64,80},{80,64},{96,112},{112,96},{1... | collective-permute-start | bytes 98312 | tf_op jit(solution)/shard_map/ppermute | solution.py:251
  74.9 0.6 shard_map.41
  75.5 0.3 collective-permute-done.2
  75.8 0.1 pad_maximum_fusion
  75.9 14.6 %all_to_all.17 = f32[32,1,512]{2,1,0:T(1,128)S(1)} all-to-all(f32[32,1,512]{2,1,0:T(1,128)S(1)} %pad_maximum_fusion), channel_id=1, replica_groups={{26,31,29,27,18,30,22,23,16,25,21,20,24,17,19,28,42,47,45,43,34,46,38,3..., dimensions={0} | all-to-all | bytes 131072 | tf_op jit(solution)/shard_map/all_to_all | solution.py:267
  90.5 0.1 reduce_max.9
  90.6 0.6 maximum_select_fusion
  (3 shorter events, 0.1 us)
Async XLA Ops:
  0.7 1.2 %copy-start = (bf16[512,1024]{1,0:T(8,128)(2,1)S(1)}, bf16[512,1024]{1,0:T(8,128)(2,1)}, u32[]{:S(2)}) copy-start(bf16[512,1024]{1,0:T(8,128)(2,1)} %doc_ref.1) | copy-start | bytes 3145732
  1.9 0.7 copy-start.1
  3.6 22.6 %copy-start.2 = (s32[1,4]{1,0:T(1,128)S(1)}, s32[1,4]{1,0:T(1,128)}, u32[]{:S(2)}) copy-start(s32[1,4]{1,0:T(1,128)} %partners_ref.1) | copy-start | bytes 52
  26.2 2.8 %collective-permute-start = (bf16[16,272,128]{2,1,0:T(8,128)(2,1)S(1)}, bf16[16,272,128]{2,1,0:T(8,128)(2,1)S(1)}, u32[]{:S(2)}, u32[]{:S(2)}) collective-permute-start(bf16[16,272,128]{2,1,0:T(8,128)(2,1)S(1)} %all_to_all.15.own_ref), channel_id=1, source_target_pairs={{0,16},{16,0},{32,48},{48,32},{64,80},{80,64},{96,112},{112,96},{1... | collective-permute-start | bytes 3342344 | tf_op jit(solution)/shard_map/ppermute | solution.py:217
  28.9 0.7 collective-permute-start.1
  62.5 13.3 %collective-permute-start.2 = (f32[16,1,512]{2,1,0:T(1,128)S(1)}, f32[16,1,512]{2,1,0:T(1,128)S(1)}, u32[]{:S(2)}, u32[]{:S(2)}) collective-permute-start(f32[16,1,512]{2,1,0:T(1,128)S(1)} %get-tuple-element.36), channel_id=1, source_target_pairs={{0,16},{16,0},{32,48},{48,32},{64,80},{80,64},{96,112},{112,96},{1... | collective-permute-start | bytes 98312 | tf_op jit(solution)/shard_map/ppermute | solution.py:251

commit v8 on v7

--- a/solution.py
+++ b/solution.py
@@ -16,8 +16,8 @@
 BODY = TILES * CUT
 TALL = BODY + 16
 STEP = 256
-ORDER = [10, 15, 13, 11, 2, 14, 6, 7, 0, 9, 5, 4, 8, 1, 3, 12]
-REACH = ORDER
+ORDER = [10, 15, 13, 11, 12, 14, 6, 7, 0, 9, 5, 4, 8, 1, 3, 2]
+REACH = [10, 15, 13, 11, 2, 14, 6, 7, 0, 9, 5, 4, 8, 1, 3, 12]
 PLACE = [ORDER.index(s) for s in range(GROUP)]
 REACH_PLACE = [REACH.index(s) for s in range(GROUP)]
 VMEM = pl.BlockSpec(memory_space=pltpu.VMEM)
@@ -79,33 +79,26 @@
 
 
 def pick(table_ref, info_ref, own_ref, near_ref, far_ref, out_ref):
-    def each(body):
+    def all_from(next_ref):
         for e in range(GROUP * SLOTS):
             dst, slot = e // SLOTS, e % SLOTS
-            body(dst, slot, table_ref[dst * PAIRS + 1 + slot])
-
-    def from_own(dst, slot, code):
-        @pl.when(code < GROUP)
-        def _():
-            out_ref[dst, slot] = own_ref[code, :BODY]
-
-    def from_next(next_ref):
-        def one(dst, slot, code):
+            code = table_ref[dst * PAIRS + 1 + slot]
+
+            @pl.when(code < GROUP)
+            def _():
+                out_ref[dst, slot] = own_ref[code, :BODY]
+
             @pl.when(code >= GROUP)
             def _():
                 out_ref[dst, slot] = next_ref[code - GROUP, :BODY]
 
-        return one
-
-    each(from_own)
-
-    @pl.when(info_ref[0] == 0)
-    def _():
-        each(from_next(near_ref))
+    @pl.when(info_ref[0] == 0)
+    def _():
+        all_from(near_ref)
 
     @pl.when(info_ref[0] == 1)
     def _():
-        each(from_next(far_ref))
+        all_from(far_ref)
 
 
 def rows_of(slices):

time: 91.4 us -> 91 us (level)
  no operation moved by 1% of the time
where the time goes in v8:
time: 91 us; the launch traced here: 90.7 us
  blocking collectives  64.4 us (71%)
  starting transfers between devices  13.4 us (15%)
  Pallas kernels  7.16 us (8%)
  waiting for transfers between devices  2.27 us (2%)
  local copies, waits for them, and re-layouts  1.96 us (2%)
    all_to_all x2, blocking collectives, exchange(): lax.all_to_all(parts, 'shard', 0, 0, axis_index_groups=[ORDER], tiled=True)  50.1 us
    all_to_all x1, blocking collectives, shards(): lax.all_to_all(send, ('cluster', 'shard'), 0, 0, axis_index_groups=reach,...  14.3 us
    ppermute x1, starting transfers between devices, shards(): over = lax.ppermute(over, 'cluster', [(c, c ^ 1) for c in range(n_cluster)])  12.6 us
    pallas_call x1, Pallas kernels, shards(): pl.pallas_call(even_scores, in_specs=[SMEM, VMEM, VMEM], out_specs=[VMEM]...  3.64 us
    ppermute x1, waiting for transfers between devices, shards(): near = lax.ppermute(own, 'cluster', [(c, c ^ 1) for c in range(n_cluster)])  1.98 us
    unnamed x6, local copies, waits for them, and re-layouts  1.88 us
  transfers between devices with their start and end apart: 3, of which 2 were waited for; matrix products, arithmetic and copies ran while one was open for 0% of the time, Pallas kernels for 1%

profile of v8, /device:TPU:0, one launch (start us, length us, event | category | flops | bytes accessed | tf_op | source)
XLA Modules:
  0.0 90.7 jit_solution(2936381158653675920)
XLA Ops:
  0.7 0.0 copy-start
  0.7 1.2 %copy-done = bf16[512,1024]{1,0:T(8,128)(2,1)S(1)} copy-done((bf16[512,1024]{1,0:T(8,128)(2,1)S(1)}, bf16[512,1024]{1,0:T(8,128)(2,1)}, u32[]{:S(2)}) %copy-start) | copy-done | bytes 1048600
  1.9 0.7 copy-done.1
  2.5 1.1 %shard_map.37.unit_ref = bf16[16,272,128]{2,1,0:T(8,128)(2,1)S(1)} custom-call(s32[1,4]{1,0:T(1,128)S(1)} %copy-done.1, s32[1]{0:T(128)} %copy.8.counts_ref, bf16[512,1024]{1,0:T(8,128)(2,1)S(1)} %copy-done), custom_call_target="tpu_custom_call" | custom-call | tf_op jit(solution)/shard_map/pallas_call | solution.py:195
  3.6 0.0 copy-start.2
  3.6 22.5 %all_to_all.15.own_ref = bf16[16,272,128]{2,1,0:T(8,128)(2,1)S(1)} all-to-all(bf16[16,272,128]{2,1,0:T(8,128)(2,1)S(1)} %shard_map.37.unit_ref), channel_id=1, replica_groups={{10,15,13,11,12,14,6,7,0,9,5,4,8,1,3,2},{26,31,29,27,28,30,22,23,16,25,..., dimensions={0} | all-to-all | bytes 2228224 | tf_op jit(solution)/shard_map/all_to_all | solution.py:188
  26.2 0.0 collective-permute-start
  26.2 0.0 copy-done.2
  26.2 0.1 pad_add_fusion.info_ref
  26.3 0.1 reshape.4.table_ref
  26.4 0.6 shard_map.38.self_ref
  26.9 2.0 %collective-permute-done.near_ref = bf16[16,272,128]{2,1,0:T(8,128)(2,1)S(1)} collective-permute-done((bf16[16,272,128]{2,1,0:T(8,128)(2,1)S(1)}, bf16[16,272,128]{2,1,0:T(8,128)(2,1)S(1)}, u32[]{:S(2)}, u32[]{:S(2)}) %collective-permute-start) | collective-permute-done | bytes 1114144 | tf_op jit(solution)/shard_map/ppermute | solution.py:210
  28.9 0.7 collective-permute-start.1
  29.6 0.0 collective-permute-done.1.far_ref
  29.6 1.3 %shard_map.39 = bf16[16,3,256,128]{3,2,1,0:T(8,128)(2,1)S(1)} custom-call(s32[64]{0:T(128)S(1)} %reshape.4.table_ref, s32[7]{0:T(128)S(1)} %pad_add_fusion.info_ref, bf16[16,272,128]{2,1,0:T(8,128)(2,1)S(1)} %all_to_all.15.own_ref, bf16[16,272,128]{2,1,0:T(8,128)(2,1)S(1)} %collective-permute-done.near_ref, ...), custom_call_target="tpu_custom_call" | custom-call | tf_op jit(solution)/shard_map/pallas_call | solution.py:224
  31.0 27.6 %all_to_all.16.got_ref = bf16[16,3,256,128]{3,2,1,0:T(8,128)(2,1)S(1)} all-to-all(bf16[16,3,256,128]{3,2,1,0:T(8,128)(2,1)S(1)} %shard_map.39), channel_id=1, replica_groups={{10,15,13,11,12,14,6,7,0,9,5,4,8,1,3,2},{26,31,29,27,28,30,22,23,16,25,..., dimensions={0} | all-to-all | bytes 6291456 | tf_op jit(solution)/shard_map/all_to_all | solution.py:188
  58.6 3.6 %shard_map.40 = (f32[1,512]{1,0:T(1,128)S(1)}, f32[32,1,512]{2,1,0:T(1,128)S(1)}, f32[16,1,512]{2,1,0:T(1,128)S(1)}) custom-call(s32[7]{0:T(128)S(1)} %pad_add_fusion.info_ref, bf16[16,272,128]{2,1,0:T(8,128)(2,1)S(1)} %shard_map.37.unit_ref, bf16[16,3,256,128]{3,2,1,0:T(8,128)(2,1)S(1)} %all_to_all.16.got_ref), custom_call_target="tpu_custom_call" | custom-call | tf_op jit(solution)/shard_map/pallas_call | solution.py:237
  62.2 12.6 %collective-permute-start.2 = (f32[16,1,512]{2,1,0:T(1,128)S(1)}, f32[16,1,512]{2,1,0:T(1,128)S(1)}, u32[]{:S(2)}, u32[]{:S(2)}) collective-permute-start(f32[16,1,512]{2,1,0:T(1,128)S(1)} %get-tuple-element.36), channel_id=1, source_target_pairs={{0,16},{16,0},{32,48},{48,32},{64,80},{80,64},{96,112},{112,96},{1... | collective-permute-start | bytes 98312 | tf_op jit(solution)/shard_map/ppermute | solution.py:244
  74.8 0.6 shard_map.41
  75.4 0.3 collective-permute-done.2
  75.7 0.1 pad_maximum_fusion
  75.8 14.3 %all_to_all.17 = f32[32,1,512]{2,1,0:T(1,128)S(1)} all-to-all(f32[32,1,512]{2,1,0:T(1,128)S(1)} %pad_maximum_fusion), channel_id=1, replica_groups={{26,31,29,27,18,30,22,23,16,25,21,20,24,17,19,28,42,47,45,43,34,46,38,3..., dimensions={0} | all-to-all | bytes 131072 | tf_op jit(solution)/shard_map/all_to_all | solution.py:260
  90.1 0.1 reduce_max.9
  90.2 0.6 maximum_select_fusion
  (3 shorter events, 0.1 us)
Async XLA Ops:
  0.7 1.2 %copy-start = (bf16[512,1024]{1,0:T(8,128)(2,1)S(1)}, bf16[512,1024]{1,0:T(8,128)(2,1)}, u32[]{:S(2)}) copy-start(bf16[512,1024]{1,0:T(8,128)(2,1)} %doc_ref.1) | copy-start | bytes 3145732
  1.9 0.7 copy-start.1
  3.6 22.6 %copy-start.2 = (s32[1,4]{1,0:T(1,128)S(1)}, s32[1,4]{1,0:T(1,128)}, u32[]{:S(2)}) copy-start(s32[1,4]{1,0:T(1,128)} %partners_ref.1) | copy-start | bytes 52
  26.2 2.8 %collective-permute-start = (bf16[16,272,128]{2,1,0:T(8,128)(2,1)S(1)}, bf16[16,272,128]{2,1,0:T(8,128)(2,1)S(1)}, u32[]{:S(2)}, u32[]{:S(2)}) collective-permute-start(bf16[16,272,128]{2,1,0:T(8,128)(2,1)S(1)} %all_to_all.15.own_ref), channel_id=1, source_target_pairs={{0,16},{16,0},{32,48},{48,32},{64,80},{80,64},{96,112},{112,96},{1... | collective-permute-start | bytes 3342344 | tf_op jit(solution)/shard_map/ppermute | solution.py:210
  28.9 0.7 collective-permute-start.1
  62.2 13.5 %collective-permute-start.2 = (f32[16,1,512]{2,1,0:T(1,128)S(1)}, f32[16,1,512]{2,1,0:T(1,128)S(1)}, u32[]{:S(2)}, u32[]{:S(2)}) collective-permute-start(f32[16,1,512]{2,1,0:T(1,128)S(1)} %get-tuple-element.36), channel_id=1, source_target_pairs={{0,16},{16,0},{32,48},{48,32},{64,80},{80,64},{96,112},{112,96},{1... | collective-permute-start | bytes 98312 | tf_op jit(solution)/shard_map/ppermute | solution.py:244

commit v9 on v8

--- a/solution.py
+++ b/solution.py
@@ -14,7 +14,7 @@
 LANES = 128
 TILES = D // LANES
 BODY = TILES * CUT
-TALL = BODY + 16
+TALL = BODY + 8
 STEP = 256
 ORDER = [10, 15, 13, 11, 12, 14, 6, 7, 0, 9, 5, 4, 8, 1, 3, 2]
 REACH = [10, 15, 13, 11, 2, 14, 6, 7, 0, 9, 5, 4, 8, 1, 3, 12]
@@ -59,7 +59,7 @@
         copy.start()
     for copy in small:
         copy.wait()
-    lane = lax.broadcasted_iota(jnp.int32, (16, LANES), 1)
+    lane = lax.broadcasted_iota(jnp.int32, (TALL - BODY, LANES), 1)
     entry = jnp.where(lane == 0, by_place(partners[0, 0]), 0)
     for p in range(1, PAIRS):
         entry = jnp.where(lane == p, by_place(partners[0, p]), entry)

time: 91 us -> 90.8 us (level)
  no operation moved by 1% of the time
where the time goes in v9:
time: 90.8 us; the launch traced here: 90.5 us
  blocking collectives  64.5 us (71%)
  starting transfers between devices  13.1 us (14%)
  Pallas kernels  7.15 us (8%)
  waiting for transfers between devices  2.22 us (2%)
  local copies, waits for them, and re-layouts  1.96 us (2%)
    all_to_all x2, blocking collectives, exchange(): lax.all_to_all(parts, 'shard', 0, 0, axis_index_groups=[ORDER], tiled=True)  50.2 us
    all_to_all x1, blocking collectives, shards(): lax.all_to_all(send, ('cluster', 'shard'), 0, 0, axis_index_groups=reach,...  14.3 us
    ppermute x1, starting transfers between devices, shards(): over = lax.ppermute(over, 'cluster', [(c, c ^ 1) for c in range(n_cluster)])  12.4 us
    pallas_call x1, Pallas kernels, shards(): pl.pallas_call(even_scores, in_specs=[SMEM, VMEM, VMEM], out_specs=[VMEM]...  3.63 us
    ppermute x1, waiting for transfers between devices, shards(): near = lax.ppermute(own, 'cluster', [(c, c ^ 1) for c in range(n_cluster)])  1.93 us
    unnamed x6, local copies, waits for them, and re-layouts  1.88 us
  transfers between devices with their start and end apart: 3, of which 2 were waited for; matrix products, arithmetic and copies ran while one was open for 0% of the time, Pallas kernels for 1%

profile of v9, /device:TPU:0, one launch (start us, length us, event | category | flops | bytes accessed | tf_op | source)
XLA Modules:
  0.0 90.5 jit_solution(16477180260126682865)
XLA Ops:
  0.7 0.0 copy-start
  0.7 1.2 %copy-done = bf16[512,1024]{1,0:T(8,128)(2,1)S(1)} copy-done((bf16[512,1024]{1,0:T(8,128)(2,1)S(1)}, bf16[512,1024]{1,0:T(8,128)(2,1)}, u32[]{:S(2)}) %copy-start) | copy-done | bytes 1048600
  1.9 0.7 copy-done.1
  2.5 1.1 %shard_map.37.unit_ref = bf16[16,264,128]{2,1,0:T(8,128)(2,1)S(1)} custom-call(s32[1,4]{1,0:T(1,128)S(1)} %copy-done.1, s32[1]{0:T(128)} %copy.8.counts_ref, bf16[512,1024]{1,0:T(8,128)(2,1)S(1)} %copy-done), custom_call_target="tpu_custom_call" | custom-call | tf_op jit(solution)/shard_map/pallas_call | solution.py:195
  3.6 0.0 copy-start.2
  3.6 22.2 %all_to_all.15.own_ref = bf16[16,264,128]{2,1,0:T(8,128)(2,1)S(1)} all-to-all(bf16[16,264,128]{2,1,0:T(8,128)(2,1)S(1)} %shard_map.37.unit_ref), channel_id=1, replica_groups={{10,15,13,11,12,14,6,7,0,9,5,4,8,1,3,2},{26,31,29,27,28,30,22,23,16,25,..., dimensions={0} | all-to-all | bytes 2162688 | tf_op jit(solution)/shard_map/all_to_all | solution.py:188
  25.9 0.0 collective-permute-start
  25.9 0.0 copy-done.2
  25.9 0.1 pad_add_fusion.info_ref
  26.0 0.1 reshape.4.table_ref
  26.1 0.6 shard_map.38.self_ref
  26.6 1.9 %collective-permute-done.near_ref = bf16[16,264,128]{2,1,0:T(8,128)(2,1)S(1)} collective-permute-done((bf16[16,264,128]{2,1,0:T(8,128)(2,1)S(1)}, bf16[16,264,128]{2,1,0:T(8,128)(2,1)S(1)}, u32[]{:S(2)}, u32[]{:S(2)}) %collective-permute-start) | collective-permute-done | bytes 1081376 | tf_op jit(solution)/shard_map/ppermute | solution.py:210
  28.6 0.7 collective-permute-start.1
  29.3 0.0 collective-permute-done.1.far_ref
  29.3 1.3 %shard_map.39 = bf16[16,3,256,128]{3,2,1,0:T(8,128)(2,1)S(1)} custom-call(s32[64]{0:T(128)S(1)} %reshape.4.table_ref, s32[7]{0:T(128)S(1)} %pad_add_fusion.info_ref, bf16[16,264,128]{2,1,0:T(8,128)(2,1)S(1)} %all_to_all.15.own_ref, bf16[16,264,128]{2,1,0:T(8,128)(2,1)S(1)} %collective-permute-done.near_ref, ...), custom_call_target="tpu_custom_call" | custom-call | tf_op jit(solution)/shard_map/pallas_call | solution.py:224
  30.7 27.9 %all_to_all.16.got_ref = bf16[16,3,256,128]{3,2,1,0:T(8,128)(2,1)S(1)} all-to-all(bf16[16,3,256,128]{3,2,1,0:T(8,128)(2,1)S(1)} %shard_map.39), channel_id=1, replica_groups={{10,15,13,11,12,14,6,7,0,9,5,4,8,1,3,2},{26,31,29,27,28,30,22,23,16,25,..., dimensions={0} | all-to-all | bytes 6291456 | tf_op jit(solution)/shard_map/all_to_all | solution.py:188
  58.6 3.6 %shard_map.40 = (f32[1,512]{1,0:T(1,128)S(1)}, f32[32,1,512]{2,1,0:T(1,128)S(1)}, f32[16,1,512]{2,1,0:T(1,128)S(1)}) custom-call(s32[7]{0:T(128)S(1)} %pad_add_fusion.info_ref, bf16[16,264,128]{2,1,0:T(8,128)(2,1)S(1)} %shard_map.37.unit_ref, bf16[16,3,256,128]{3,2,1,0:T(8,128)(2,1)S(1)} %all_to_all.16.got_ref), custom_call_target="tpu_custom_call" | custom-call | tf_op jit(solution)/shard_map/pallas_call | solution.py:237
  62.2 12.4 %collective-permute-start.2 = (f32[16,1,512]{2,1,0:T(1,128)S(1)}, f32[16,1,512]{2,1,0:T(1,128)S(1)}, u32[]{:S(2)}, u32[]{:S(2)}) collective-permute-start(f32[16,1,512]{2,1,0:T(1,128)S(1)} %get-tuple-element.36), channel_id=1, source_target_pairs={{0,16},{16,0},{32,48},{48,32},{64,80},{80,64},{96,112},{112,96},{1... | collective-permute-start | bytes 98312 | tf_op jit(solution)/shard_map/ppermute | solution.py:244
  74.6 0.6 shard_map.41
  75.2 0.3 collective-permute-done.2
  75.5 0.1 pad_maximum_fusion
  75.5 14.3 %all_to_all.17 = f32[32,1,512]{2,1,0:T(1,128)S(1)} all-to-all(f32[32,1,512]{2,1,0:T(1,128)S(1)} %pad_maximum_fusion), channel_id=1, replica_groups={{26,31,29,27,18,30,22,23,16,25,21,20,24,17,19,28,42,47,45,43,34,46,38,3..., dimensions={0} | all-to-all | bytes 131072 | tf_op jit(solution)/shard_map/all_to_all | solution.py:260
  89.9 0.1 reduce_max.9
  89.9 0.6 maximum_select_fusion
  (3 shorter events, 0.1 us)
Async XLA Ops:
  0.7 1.2 %copy-start = (bf16[512,1024]{1,0:T(8,128)(2,1)S(1)}, bf16[512,1024]{1,0:T(8,128)(2,1)}, u32[]{:S(2)}) copy-start(bf16[512,1024]{1,0:T(8,128)(2,1)} %doc_ref.1) | copy-start | bytes 3145732
  1.9 0.7 copy-start.1
  3.6 22.3 %copy-start.2 = (s32[1,4]{1,0:T(1,128)S(1)}, s32[1,4]{1,0:T(1,128)}, u32[]{:S(2)}) copy-start(s32[1,4]{1,0:T(1,128)} %partners_ref.1) | copy-start | bytes 52
  25.9 2.7 %collective-permute-start = (bf16[16,264,128]{2,1,0:T(8,128)(2,1)S(1)}, bf16[16,264,128]{2,1,0:T(8,128)(2,1)S(1)}, u32[]{:S(2)}, u32[]{:S(2)}) collective-permute-start(bf16[16,264,128]{2,1,0:T(8,128)(2,1)S(1)} %all_to_all.15.own_ref), channel_id=1, source_target_pairs={{0,16},{16,0},{32,48},{48,32},{64,80},{80,64},{96,112},{112,96},{1... | collective-permute-start | bytes 3244040 | tf_op jit(solution)/shard_map/ppermute | solution.py:210
  28.6 0.7 collective-permute-start.1
  62.2 13.3 %collective-permute-start.2 = (f32[16,1,512]{2,1,0:T(1,128)S(1)}, f32[16,1,512]{2,1,0:T(1,128)S(1)}, u32[]{:S(2)}, u32[]{:S(2)}) collective-permute-start(f32[16,1,512]{2,1,0:T(1,128)S(1)} %get-tuple-element.36), channel_id=1, source_target_pairs={{0,16},{16,0},{32,48},{48,32},{64,80},{80,64},{96,112},{112,96},{1... | collective-permute-start | bytes 98312 | tf_op jit(solution)/shard_map/ppermute | solution.py:244

commit v10 on v9

--- a/solution.py
+++ b/solution.py
@@ -14,7 +14,8 @@
 LANES = 128
 TILES = D // LANES
 BODY = TILES * CUT
-TALL = BODY + 8
+LIST = 8
+TALL = BODY + LIST
 STEP = 256
 ORDER = [10, 15, 13, 11, 12, 14, 6, 7, 0, 9, 5, 4, 8, 1, 3, 2]
 REACH = [10, 15, 13, 11, 2, 14, 6, 7, 0, 9, 5, 4, 8, 1, 3, 12]
@@ -59,7 +60,7 @@
         copy.start()
     for copy in small:
         copy.wait()
-    lane = lax.broadcasted_iota(jnp.int32, (TALL - BODY, LANES), 1)
+    lane = lax.broadcasted_iota(jnp.int32, (LIST, LANES), 1)
     entry = jnp.where(lane == 0, by_place(partners[0, 0]), 0)
     for p in range(1, PAIRS):
         entry = jnp.where(lane == p, by_place(partners[0, p]), entry)
@@ -75,7 +76,8 @@
             at = (i + j) // CUT
             for t in range(TILES):
                 unit[at, t * CUT : (t + 1) * CUT] = rows[j : j + CUT, t * LANES : (t + 1) * LANES]
-            unit[at, BODY:] = entry
+            last = rows[j + CUT - (16 - LIST) : j + CUT, D - LANES :]
+            unit[at, TALL - 16 :] = jnp.concatenate([last, entry])
 
 
 def pick(table_ref, info_ref, own_ref, near_ref, far_ref, out_ref):

time: 90.8 us -> 90.8 us (level)
  no operation moved by 1% of the time
where the time goes in v10:
time: 90.8 us; the launch traced here: 90.5 us
  blocking collectives  64.5 us (71%)
  starting transfers between devices  13.1 us (14%)
  Pallas kernels  7.17 us (8%)
  waiting for transfers between devices  2.22 us (2%)
  local copies, waits for them, and re-layouts  1.96 us (2%)
    all_to_all x2, blocking collectives, exchange(): lax.all_to_all(parts, 'shard', 0, 0, axis_index_groups=[ORDER], tiled=True)  50.2 us
    all_to_all x1, blocking collectives, shards(): lax.all_to_all(send, ('cluster', 'shard'), 0, 0, axis_index_groups=reach,...  14.3 us
    ppermute x1, starting transfers between devices, shards(): over = lax.ppermute(over, 'cluster', [(c, c ^ 1) for c in range(n_cluster)])  12.4 us
    pallas_call x1, Pallas kernels, shards(): pl.pallas_call(even_scores, in_specs=[SMEM, VMEM, VMEM], out_specs=[VMEM]...  3.63 us
    ppermute x1, waiting for transfers between devices, shards(): near = lax.ppermute(own, 'cluster', [(c, c ^ 1) for c in range(n_cluster)])  1.93 us
    unnamed x6, local copies, waits for them, and re-layouts  1.88 us
  transfers between devices with their start and end apart: 3, of which 2 were waited for; matrix products, arithmetic and copies ran while one was open for 0% of the time, Pallas kernels for 1%

profile of v10, /device:TPU:0, one launch (start us, length us, event | category | flops | bytes accessed | tf_op | source)
XLA Modules:
  0.0 90.5 jit_solution(12895243551491866914)
XLA Ops:
  0.7 0.0 copy-start
  0.7 1.2 %copy-done = bf16[512,1024]{1,0:T(8,128)(2,1)S(1)} copy-done((bf16[512,1024]{1,0:T(8,128)(2,1)S(1)}, bf16[512,1024]{1,0:T(8,128)(2,1)}, u32[]{:S(2)}) %copy-start) | copy-done | bytes 1048600
  1.9 0.7 copy-done.1
  2.5 1.1 %shard_map.37.unit_ref = bf16[16,264,128]{2,1,0:T(8,128)(2,1)S(1)} custom-call(s32[1,4]{1,0:T(1,128)S(1)} %copy-done.1, s32[1]{0:T(128)} %copy.8.counts_ref, bf16[512,1024]{1,0:T(8,128)(2,1)S(1)} %copy-done), custom_call_target="tpu_custom_call" | custom-call | tf_op jit(solution)/shard_map/pallas_call | solution.py:197
  3.6 0.0 copy-start.2
  3.6 22.2 %all_to_all.15.own_ref = bf16[16,264,128]{2,1,0:T(8,128)(2,1)S(1)} all-to-all(bf16[16,264,128]{2,1,0:T(8,128)(2,1)S(1)} %shard_map.37.unit_ref), channel_id=1, replica_groups={{10,15,13,11,12,14,6,7,0,9,5,4,8,1,3,2},{26,31,29,27,28,30,22,23,16,25,..., dimensions={0} | all-to-all | bytes 2162688 | tf_op jit(solution)/shard_map/all_to_all | solution.py:190
  25.9 0.0 collective-permute-start
  25.9 0.0 copy-done.2
  25.9 0.1 pad_add_fusion.info_ref
  26.0 0.1 reshape.4.table_ref
  26.1 0.6 shard_map.38.self_ref
  26.7 1.9 %collective-permute-done.near_ref = bf16[16,264,128]{2,1,0:T(8,128)(2,1)S(1)} collective-permute-done((bf16[16,264,128]{2,1,0:T(8,128)(2,1)S(1)}, bf16[16,264,128]{2,1,0:T(8,128)(2,1)S(1)}, u32[]{:S(2)}, u32[]{:S(2)}) %collective-permute-start) | collective-permute-done | bytes 1081376 | tf_op jit(solution)/shard_map/ppermute | solution.py:212
  28.6 0.7 collective-permute-start.1
  29.3 0.0 collective-permute-done.1.far_ref
  29.3 1.3 %shard_map.39 = bf16[16,3,256,128]{3,2,1,0:T(8,128)(2,1)S(1)} custom-call(s32[64]{0:T(128)S(1)} %reshape.4.table_ref, s32[7]{0:T(128)S(1)} %pad_add_fusion.info_ref, bf16[16,264,128]{2,1,0:T(8,128)(2,1)S(1)} %all_to_all.15.own_ref, bf16[16,264,128]{2,1,0:T(8,128)(2,1)S(1)} %collective-permute-done.near_ref, ...), custom_call_target="tpu_custom_call" | custom-call | tf_op jit(solution)/shard_map/pallas_call | solution.py:226
  30.7 27.9 %all_to_all.16.got_ref = bf16[16,3,256,128]{3,2,1,0:T(8,128)(2,1)S(1)} all-to-all(bf16[16,3,256,128]{3,2,1,0:T(8,128)(2,1)S(1)} %shard_map.39), channel_id=1, replica_groups={{10,15,13,11,12,14,6,7,0,9,5,4,8,1,3,2},{26,31,29,27,28,30,22,23,16,25,..., dimensions={0} | all-to-all | bytes 6291456 | tf_op jit(solution)/shard_map/all_to_all | solution.py:190
  58.6 3.6 %shard_map.40 = (f32[1,512]{1,0:T(1,128)S(1)}, f32[32,1,512]{2,1,0:T(1,128)S(1)}, f32[16,1,512]{2,1,0:T(1,128)S(1)}) custom-call(s32[7]{0:T(128)S(1)} %pad_add_fusion.info_ref, bf16[16,264,128]{2,1,0:T(8,128)(2,1)S(1)} %shard_map.37.unit_ref, bf16[16,3,256,128]{3,2,1,0:T(8,128)(2,1)S(1)} %all_to_all.16.got_ref), custom_call_target="tpu_custom_call" | custom-call | tf_op jit(solution)/shard_map/pallas_call | solution.py:239
  62.2 12.4 %collective-permute-start.2 = (f32[16,1,512]{2,1,0:T(1,128)S(1)}, f32[16,1,512]{2,1,0:T(1,128)S(1)}, u32[]{:S(2)}, u32[]{:S(2)}) collective-permute-start(f32[16,1,512]{2,1,0:T(1,128)S(1)} %get-tuple-element.36), channel_id=1, source_target_pairs={{0,16},{16,0},{32,48},{48,32},{64,80},{80,64},{96,112},{112,96},{1... | collective-permute-start | bytes 98312 | tf_op jit(solution)/shard_map/ppermute | solution.py:246
  74.6 0.6 shard_map.41
  75.2 0.3 collective-permute-done.2
  75.5 0.1 pad_maximum_fusion
  75.6 14.3 %all_to_all.17 = f32[32,1,512]{2,1,0:T(1,128)S(1)} all-to-all(f32[32,1,512]{2,1,0:T(1,128)S(1)} %pad_maximum_fusion), channel_id=1, replica_groups={{26,31,29,27,18,30,22,23,16,25,21,20,24,17,19,28,42,47,45,43,34,46,38,3..., dimensions={0} | all-to-all | bytes 131072 | tf_op jit(solution)/shard_map/all_to_all | solution.py:262
  89.9 0.1 reduce_max.9
  90.0 0.6 maximum_select_fusion
  (3 shorter events, 0.1 us)
Async XLA Ops:
  0.7 1.2 %copy-start = (bf16[512,1024]{1,0:T(8,128)(2,1)S(1)}, bf16[512,1024]{1,0:T(8,128)(2,1)}, u32[]{:S(2)}) copy-start(bf16[512,1024]{1,0:T(8,128)(2,1)} %doc_ref.1) | copy-start | bytes 3145732
  1.9 0.7 copy-start.1
  3.6 22.3 %copy-start.2 = (s32[1,4]{1,0:T(1,128)S(1)}, s32[1,4]{1,0:T(1,128)}, u32[]{:S(2)}) copy-start(s32[1,4]{1,0:T(1,128)} %partners_ref.1) | copy-start | bytes 52
  25.9 2.7 %collective-permute-start = (bf16[16,264,128]{2,1,0:T(8,128)(2,1)S(1)}, bf16[16,264,128]{2,1,0:T(8,128)(2,1)S(1)}, u32[]{:S(2)}, u32[]{:S(2)}) collective-permute-start(bf16[16,264,128]{2,1,0:T(8,128)(2,1)S(1)} %all_to_all.15.own_ref), channel_id=1, source_target_pairs={{0,16},{16,0},{32,48},{48,32},{64,80},{80,64},{96,112},{112,96},{1... | collective-permute-start | bytes 3244040 | tf_op jit(solution)/shard_map/ppermute | solution.py:212
  28.6 0.7 collective-permute-start.1
  62.2 13.3 %collective-permute-start.2 = (f32[16,1,512]{2,1,0:T(1,128)S(1)}, f32[16,1,512]{2,1,0:T(1,128)S(1)}, u32[]{:S(2)}, u32[]{:S(2)}) collective-permute-start(f32[16,1,512]{2,1,0:T(1,128)S(1)} %get-tuple-element.36), channel_id=1, source_target_pairs={{0,16},{16,0},{32,48},{48,32},{64,80},{80,64},{96,112},{112,96},{1... | collective-permute-start | bytes 98312 | tf_op jit(solution)/shard_map/ppermute | solution.py:246

commit v11 on v10

--- a/solution.py
+++ b/solution.py
@@ -47,16 +47,12 @@
     return raw * lax.rsqrt(jnp.sum(raw * raw, axis=1, keepdims=True) + 1e-06)
 
 
-def normalise(partners_ref, counts_ref, doc_ref, unit, raw, partners, counts, in_sem, small_sem):
+def normalise(partners_ref, counts_ref, doc_ref, unit, partners, counts, small_sem):
     small = [
         pltpu.make_async_copy(partners_ref, partners, small_sem.at[0]),
         pltpu.make_async_copy(counts_ref, counts, small_sem.at[1]),
     ]
-    fetch = [
-        pltpu.make_async_copy(doc_ref.at[pl.ds(i, STEP)], raw.at[pl.ds(i, STEP)], in_sem.at[i // STEP])
-        for i in range(0, ROWS, STEP)
-    ]
-    for copy in small + fetch:
+    for copy in small:
         copy.start()
     for copy in small:
         copy.wait()
@@ -66,8 +62,7 @@
         entry = jnp.where(lane == p, by_place(partners[0, p]), entry)
     entry = entry.astype(jnp.float32).astype(jnp.bfloat16)
     for i in range(0, ROWS, STEP):
-        fetch[i // STEP].wait()
-        rows = unit_rows(raw[i : i + STEP])
+        rows = unit_rows(doc_ref[i : i + STEP])
         if i == 0:
             first = rows[:1]
         row = i + lax.broadcasted_iota(jnp.int32, (STEP, 1), 0)
@@ -196,14 +191,12 @@
     odd = my_cluster % 2
     unit = pl.pallas_call(
         normalise,
-        in_specs=[ANY] * 3,
+        in_specs=[ANY, ANY, VMEM],
         out_specs=VMEM,
         out_shape=jax.ShapeDtypeStruct((GROUP, TALL, LANES), jnp.bfloat16),
         scratch_shapes=[
-            pltpu.VMEM((ROWS, D), jnp.bfloat16),
             pltpu.SMEM((1, PAIRS), jnp.int32),
             pltpu.SMEM((1,), jnp.int32),
-            pltpu.SemaphoreType.DMA((ROWS // STEP,)),
             pltpu.SemaphoreType.DMA((2,)),
         ],
         compiler_params=pltpu.CompilerParams(vmem_limit_bytes=8 * 2**20),

time: 90.8 us -> 90.7 us (level)
  no operation moved by 1% of the time
where the time goes in v11:
time: 90.7 us; the launch traced here: 90.4 us
  blocking collectives  64.5 us (71%)
  starting transfers between devices  13.1 us (14%)
  Pallas kernels  7.11 us (8%)
  waiting for transfers between devices  2.22 us (2%)
  local copies, waits for them, and re-layouts  1.96 us (2%)
    all_to_all x2, blocking collectives, exchange(): lax.all_to_all(parts, 'shard', 0, 0, axis_index_groups=[ORDER], tiled=True)  50.2 us
    all_to_all x1, blocking collectives, shards(): lax.all_to_all(send, ('cluster', 'shard'), 0, 0, axis_index_groups=reach,...  14.3 us
    ppermute x1, starting transfers between devices, shards(): over = lax.ppermute(over, 'cluster', [(c, c ^ 1) for c in range(n_cluster)])  12.4 us
    pallas_call x1, Pallas kernels, shards(): pl.pallas_call(even_scores, in_specs=[SMEM, VMEM, VMEM], out_specs=[VMEM]...  3.64 us
    ppermute x1, waiting for transfers between devices, shards(): near = lax.ppermute(own, 'cluster', [(c, c ^ 1) for c in range(n_cluster)])  1.93 us
    unnamed x6, local copies, waits for them, and re-layouts  1.88 us
  transfers between devices with their start and end apart: 3, of which 2 were waited for; matrix products, arithmetic and copies ran while one was open for 0% of the time, Pallas kernels for 1%

profile of v11, /device:TPU:0, one launch (start us, length us, event | category | flops | bytes accessed | tf_op | source)
XLA Modules:
  0.0 90.4 jit_solution(3296688113434363908)
XLA Ops:
  0.7 0.0 copy-start
  0.7 1.2 %copy-done = bf16[512,1024]{1,0:T(8,128)(2,1)S(1)} copy-done((bf16[512,1024]{1,0:T(8,128)(2,1)S(1)}, bf16[512,1024]{1,0:T(8,128)(2,1)}, u32[]{:S(2)}) %copy-start) | copy-done | bytes 1048600
  1.9 0.7 copy-done.1
  2.5 1.0 %shard_map.37.unit_ref = bf16[16,264,128]{2,1,0:T(8,128)(2,1)S(1)} custom-call(s32[1,4]{1,0:T(1,128)S(1)} %copy-done.1, s32[1]{0:T(128)} %copy.8.counts_ref, bf16[512,1024]{1,0:T(8,128)(2,1)S(1)} %copy-done), custom_call_target="tpu_custom_call" | custom-call | tf_op jit(solution)/shard_map/pallas_call | solution.py:192
  3.6 0.0 copy-start.2
  3.6 22.2 %all_to_all.15.own_ref = bf16[16,264,128]{2,1,0:T(8,128)(2,1)S(1)} all-to-all(bf16[16,264,128]{2,1,0:T(8,128)(2,1)S(1)} %shard_map.37.unit_ref), channel_id=1, replica_groups={{10,15,13,11,12,14,6,7,0,9,5,4,8,1,3,2},{26,31,29,27,28,30,22,23,16,25,..., dimensions={0} | all-to-all | bytes 2162688 | tf_op jit(solution)/shard_map/all_to_all | solution.py:185
  25.8 0.0 collective-permute-start
  25.8 0.0 copy-done.2
  25.8 0.1 pad_add_fusion.info_ref
  25.9 0.1 reshape.4.table_ref
  26.0 0.6 shard_map.38.self_ref
  26.6 1.9 %collective-permute-done.near_ref = bf16[16,264,128]{2,1,0:T(8,128)(2,1)S(1)} collective-permute-done((bf16[16,264,128]{2,1,0:T(8,128)(2,1)S(1)}, bf16[16,264,128]{2,1,0:T(8,128)(2,1)S(1)}, u32[]{:S(2)}, u32[]{:S(2)}) %collective-permute-start) | collective-permute-done | bytes 1081376 | tf_op jit(solution)/shard_map/ppermute | solution.py:205
  28.5 0.7 collective-permute-start.1
  29.2 0.0 collective-permute-done.1.far_ref
  29.3 1.3 %shard_map.39 = bf16[16,3,256,128]{3,2,1,0:T(8,128)(2,1)S(1)} custom-call(s32[64]{0:T(128)S(1)} %reshape.4.table_ref, s32[7]{0:T(128)S(1)} %pad_add_fusion.info_ref, bf16[16,264,128]{2,1,0:T(8,128)(2,1)S(1)} %all_to_all.15.own_ref, bf16[16,264,128]{2,1,0:T(8,128)(2,1)S(1)} %collective-permute-done.near_ref, ...), custom_call_target="tpu_custom_call" | custom-call | tf_op jit(solution)/shard_map/pallas_call | solution.py:219
  30.6 27.9 %all_to_all.16.got_ref = bf16[16,3,256,128]{3,2,1,0:T(8,128)(2,1)S(1)} all-to-all(bf16[16,3,256,128]{3,2,1,0:T(8,128)(2,1)S(1)} %shard_map.39), channel_id=1, replica_groups={{10,15,13,11,12,14,6,7,0,9,5,4,8,1,3,2},{26,31,29,27,28,30,22,23,16,25,..., dimensions={0} | all-to-all | bytes 6291456 | tf_op jit(solution)/shard_map/all_to_all | solution.py:185
  58.5 3.6 %shard_map.40 = (f32[1,512]{1,0:T(1,128)S(1)}, f32[32,1,512]{2,1,0:T(1,128)S(1)}, f32[16,1,512]{2,1,0:T(1,128)S(1)}) custom-call(s32[7]{0:T(128)S(1)} %pad_add_fusion.info_ref, bf16[16,264,128]{2,1,0:T(8,128)(2,1)S(1)} %shard_map.37.unit_ref, bf16[16,3,256,128]{3,2,1,0:T(8,128)(2,1)S(1)} %all_to_all.16.got_ref), custom_call_target="tpu_custom_call" | custom-call | tf_op jit(solution)/shard_map/pallas_call | solution.py:232
  62.1 12.4 %collective-permute-start.2 = (f32[16,1,512]{2,1,0:T(1,128)S(1)}, f32[16,1,512]{2,1,0:T(1,128)S(1)}, u32[]{:S(2)}, u32[]{:S(2)}) collective-permute-start(f32[16,1,512]{2,1,0:T(1,128)S(1)} %get-tuple-element.36), channel_id=1, source_target_pairs={{0,16},{16,0},{32,48},{48,32},{64,80},{80,64},{96,112},{112,96},{1... | collective-permute-start | bytes 98312 | tf_op jit(solution)/shard_map/ppermute | solution.py:239
  74.5 0.6 shard_map.41
  75.1 0.3 collective-permute-done.2
  75.4 0.1 pad_maximum_fusion
  75.5 14.3 %all_to_all.17 = f32[32,1,512]{2,1,0:T(1,128)S(1)} all-to-all(f32[32,1,512]{2,1,0:T(1,128)S(1)} %pad_maximum_fusion), channel_id=1, replica_groups={{26,31,29,27,18,30,22,23,16,25,21,20,24,17,19,28,42,47,45,43,34,46,38,3..., dimensions={0} | all-to-all | bytes 131072 | tf_op jit(solution)/shard_map/all_to_all | solution.py:255
  89.8 0.1 reduce_max.9
  89.9 0.6 maximum_select_fusion
  (3 shorter events, 0.1 us)
Async XLA Ops:
  0.7 1.2 %copy-start = (bf16[512,1024]{1,0:T(8,128)(2,1)S(1)}, bf16[512,1024]{1,0:T(8,128)(2,1)}, u32[]{:S(2)}) copy-start(bf16[512,1024]{1,0:T(8,128)(2,1)} %doc_ref.1) | copy-start | bytes 3145732
  1.9 0.7 copy-start.1
  3.6 22.3 %copy-start.2 = (s32[1,4]{1,0:T(1,128)S(1)}, s32[1,4]{1,0:T(1,128)}, u32[]{:S(2)}) copy-start(s32[1,4]{1,0:T(1,128)} %partners_ref.1) | copy-start | bytes 52
  25.8 2.7 %collective-permute-start = (bf16[16,264,128]{2,1,0:T(8,128)(2,1)S(1)}, bf16[16,264,128]{2,1,0:T(8,128)(2,1)S(1)}, u32[]{:S(2)}, u32[]{:S(2)}) collective-permute-start(bf16[16,264,128]{2,1,0:T(8,128)(2,1)S(1)} %all_to_all.15.own_ref), channel_id=1, source_target_pairs={{0,16},{16,0},{32,48},{48,32},{64,80},{80,64},{96,112},{112,96},{1... | collective-permute-start | bytes 3244040 | tf_op jit(solution)/shard_map/ppermute | solution.py:205
  28.5 0.7 collective-permute-start.1
  62.1 13.2 %collective-permute-start.2 = (f32[16,1,512]{2,1,0:T(1,128)S(1)}, f32[16,1,512]{2,1,0:T(1,128)S(1)}, u32[]{:S(2)}, u32[]{:S(2)}) collective-permute-start(f32[16,1,512]{2,1,0:T(1,128)S(1)} %get-tuple-element.36), channel_id=1, source_target_pairs={{0,16},{16,0},{32,48},{48,32},{64,80},{80,64},{96,112},{112,96},{1... | collective-permute-start | bytes 98312 | tf_op jit(solution)/shard_map/ppermute | solution.py:239

commit v12 on v11

--- a/solution.py
+++ b/solution.py
@@ -18,7 +18,7 @@
 TALL = BODY + LIST
 STEP = 256
 ORDER = [10, 15, 13, 11, 12, 14, 6, 7, 0, 9, 5, 4, 8, 1, 3, 2]
-REACH = [10, 15, 13, 11, 2, 14, 6, 7, 0, 9, 5, 4, 8, 1, 3, 12]
+REACH = ORDER
 PLACE = [ORDER.index(s) for s in range(GROUP)]
 REACH_PLACE = [REACH.index(s) for s in range(GROUP)]
 VMEM = pl.BlockSpec(memory_space=pltpu.VMEM)

time: 90.7 us -> 90.8 us (level)
  no operation moved by 1% of the time
where the time goes in v12:
time: 90.8 us; the launch traced here: 90.5 us
  blocking collectives  64.5 us (71%)
  starting transfers between devices  13.1 us (14%)
  Pallas kernels  7.09 us (8%)
  waiting for transfers between devices  2.22 us (2%)
  local copies, waits for them, and re-layouts  1.96 us (2%)
    all_to_all x2, blocking collectives, exchange(): lax.all_to_all(parts, 'shard', 0, 0, axis_index_groups=[ORDER], tiled=True)  50.2 us
    all_to_all x1, blocking collectives, shards(): lax.all_to_all(send, ('cluster', 'shard'), 0, 0, axis_index_groups=reach,...  14.3 us
    ppermute x1, starting transfers between devices, shards(): over = lax.ppermute(over, 'cluster', [(c, c ^ 1) for c in range(n_cluster)])  12.4 us
    pallas_call x1, Pallas kernels, shards(): pl.pallas_call(even_scores, in_specs=[SMEM, VMEM, VMEM], out_specs=[VMEM]...  3.62 us
    ppermute x1, waiting for transfers between devices, shards(): near = lax.ppermute(own, 'cluster', [(c, c ^ 1) for c in range(n_cluster)])  1.93 us
    unnamed x6, local copies, waits for them, and re-layouts  1.88 us
  transfers between devices with their start and end apart: 3, of which 2 were waited for; matrix products, arithmetic and copies ran while one was open for 0% of the time, Pallas kernels for 1%

profile of v12, /device:TPU:0, one launch (start us, length us, event | category | flops | bytes accessed | tf_op | source)
XLA Modules:
  0.0 90.5 jit_solution(4999341937869284617)
XLA Ops:
  0.7 0.0 copy-start
  0.7 1.2 %copy-done = bf16[512,1024]{1,0:T(8,128)(2,1)S(1)} copy-done((bf16[512,1024]{1,0:T(8,128)(2,1)S(1)}, bf16[512,1024]{1,0:T(8,128)(2,1)}, u32[]{:S(2)}) %copy-start) | copy-done | bytes 1048600
  1.9 0.7 copy-done.1
  2.5 1.0 %shard_map.37.unit_ref = bf16[16,264,128]{2,1,0:T(8,128)(2,1)S(1)} custom-call(s32[1,4]{1,0:T(1,128)S(1)} %copy-done.1, s32[1]{0:T(128)} %copy.8.counts_ref, bf16[512,1024]{1,0:T(8,128)(2,1)S(1)} %copy-done), custom_call_target="tpu_custom_call" | custom-call | tf_op jit(solution)/shard_map/pallas_call | solution.py:192
  3.6 0.0 copy-start.2
  3.6 22.2 %all_to_all.15.own_ref = bf16[16,264,128]{2,1,0:T(8,128)(2,1)S(1)} all-to-all(bf16[16,264,128]{2,1,0:T(8,128)(2,1)S(1)} %shard_map.37.unit_ref), channel_id=1, replica_groups={{10,15,13,11,12,14,6,7,0,9,5,4,8,1,3,2},{26,31,29,27,28,30,22,23,16,25,..., dimensions={0} | all-to-all | bytes 2162688 | tf_op jit(solution)/shard_map/all_to_all | solution.py:185
  25.8 0.0 collective-permute-start
  25.8 0.0 copy-done.2
  25.8 0.1 pad_add_fusion.info_ref
  25.9 0.1 reshape.4.table_ref
  26.0 0.6 shard_map.38.self_ref
  26.6 1.9 %collective-permute-done.near_ref = bf16[16,264,128]{2,1,0:T(8,128)(2,1)S(1)} collective-permute-done((bf16[16,264,128]{2,1,0:T(8,128)(2,1)S(1)}, bf16[16,264,128]{2,1,0:T(8,128)(2,1)S(1)}, u32[]{:S(2)}, u32[]{:S(2)}) %collective-permute-start) | collective-permute-done | bytes 1081376 | tf_op jit(solution)/shard_map/ppermute | solution.py:205
  28.5 0.7 collective-permute-start.1
  29.2 0.0 collective-permute-done.1.far_ref
  29.3 1.3 %shard_map.39 = bf16[16,3,256,128]{3,2,1,0:T(8,128)(2,1)S(1)} custom-call(s32[64]{0:T(128)S(1)} %reshape.4.table_ref, s32[7]{0:T(128)S(1)} %pad_add_fusion.info_ref, bf16[16,264,128]{2,1,0:T(8,128)(2,1)S(1)} %all_to_all.15.own_ref, bf16[16,264,128]{2,1,0:T(8,128)(2,1)S(1)} %collective-permute-done.near_ref, ...), custom_call_target="tpu_custom_call" | custom-call | tf_op jit(solution)/shard_map/pallas_call | solution.py:219
  30.6 27.9 %all_to_all.16.got_ref = bf16[16,3,256,128]{3,2,1,0:T(8,128)(2,1)S(1)} all-to-all(bf16[16,3,256,128]{3,2,1,0:T(8,128)(2,1)S(1)} %shard_map.39), channel_id=1, replica_groups={{10,15,13,11,12,14,6,7,0,9,5,4,8,1,3,2},{26,31,29,27,28,30,22,23,16,25,..., dimensions={0} | all-to-all | bytes 6291456 | tf_op jit(solution)/shard_map/all_to_all | solution.py:185
  58.5 3.6 %shard_map.40 = (f32[1,512]{1,0:T(1,128)S(1)}, f32[32,1,512]{2,1,0:T(1,128)S(1)}, f32[16,1,512]{2,1,0:T(1,128)S(1)}) custom-call(s32[7]{0:T(128)S(1)} %pad_add_fusion.info_ref, bf16[16,264,128]{2,1,0:T(8,128)(2,1)S(1)} %shard_map.37.unit_ref, bf16[16,3,256,128]{3,2,1,0:T(8,128)(2,1)S(1)} %all_to_all.16.got_ref), custom_call_target="tpu_custom_call" | custom-call | tf_op jit(solution)/shard_map/pallas_call | solution.py:232
  62.1 12.4 %collective-permute-start.2 = (f32[16,1,512]{2,1,0:T(1,128)S(1)}, f32[16,1,512]{2,1,0:T(1,128)S(1)}, u32[]{:S(2)}, u32[]{:S(2)}) collective-permute-start(f32[16,1,512]{2,1,0:T(1,128)S(1)} %get-tuple-element.36), channel_id=1, source_target_pairs={{0,16},{16,0},{32,48},{48,32},{64,80},{80,64},{96,112},{112,96},{1... | collective-permute-start | bytes 98312 | tf_op jit(solution)/shard_map/ppermute | solution.py:239
  74.5 0.6 shard_map.41
  75.1 0.3 collective-permute-done.2
  75.4 0.1 pad_maximum_fusion
  75.5 14.3 %all_to_all.17 = f32[32,1,512]{2,1,0:T(1,128)S(1)} all-to-all(f32[32,1,512]{2,1,0:T(1,128)S(1)} %pad_maximum_fusion), channel_id=1, replica_groups={{26,31,29,27,28,30,22,23,16,25,21,20,24,17,19,18,42,47,45,43,44,46,38,3..., dimensions={0} | all-to-all | bytes 131072 | tf_op jit(solution)/shard_map/all_to_all | solution.py:255
  89.8 0.1 reduce_max.9
  89.9 0.6 maximum_select_fusion
  (3 shorter events, 0.1 us)
Async XLA Ops:
  0.7 1.2 %copy-start = (bf16[512,1024]{1,0:T(8,128)(2,1)S(1)}, bf16[512,1024]{1,0:T(8,128)(2,1)}, u32[]{:S(2)}) copy-start(bf16[512,1024]{1,0:T(8,128)(2,1)} %doc_ref.1) | copy-start | bytes 3145732
  1.9 0.7 copy-start.1
  3.6 22.3 %copy-start.2 = (s32[1,4]{1,0:T(1,128)S(1)}, s32[1,4]{1,0:T(1,128)}, u32[]{:S(2)}) copy-start(s32[1,4]{1,0:T(1,128)} %partners_ref.1) | copy-start | bytes 52
  25.8 2.7 %collective-permute-start = (bf16[16,264,128]{2,1,0:T(8,128)(2,1)S(1)}, bf16[16,264,128]{2,1,0:T(8,128)(2,1)S(1)}, u32[]{:S(2)}, u32[]{:S(2)}) collective-permute-start(bf16[16,264,128]{2,1,0:T(8,128)(2,1)S(1)} %all_to_all.15.own_ref), channel_id=1, source_target_pairs={{0,16},{16,0},{32,48},{48,32},{64,80},{80,64},{96,112},{112,96},{1... | collective-permute-start | bytes 3244040 | tf_op jit(solution)/shard_map/ppermute | solution.py:205
  28.5 0.7 collective-permute-start.1
  62.1 13.3 %collective-permute-start.2 = (f32[16,1,512]{2,1,0:T(1,128)S(1)}, f32[16,1,512]{2,1,0:T(1,128)S(1)}, u32[]{:S(2)}, u32[]{:S(2)}) collective-permute-start(f32[16,1,512]{2,1,0:T(1,128)S(1)} %get-tuple-element.36), channel_id=1, source_target_pairs={{0,16},{16,0},{32,48},{48,32},{64,80},{80,64},{96,112},{112,96},{1... | collective-permute-start | bytes 98312 | tf_op jit(solution)/shard_map/ppermute | solution.py:239
